TPU v7x, 256 devices: a whole 4x4x8 slice. The times are simulated.
256 devices in a mesh: seq: 64 (over y, z, core), tp: 4 (over x).
Axes of the slice: x: 4, y: 4, z: 8, core: 2. Of those that a mesh axis runs over, the one named last changes fastest.
Arguments:
- tokens: int32 [8192], P('seq'), may hold values from 0 to 511
- table: bfloat16 [512, 3, 4096], P(None, None, 'tp'), may hold values from -6 to 6
- short_kernel: float32 [3, 3, 4096], P(None, None, 'tp'), may hold values from -4 to 4
- poles: float32 [16, 4096], P(None, 'tp'), may hold values from 0 to 1, as said below
- residues: float32 [16, 4096], P(None, 'tp'), may hold values from -1 to 1
- skip: float32 [4096], P('tp'), may hold values from -4 to 4
- out_weight: bfloat16 [4096, 4096], P(('tp', 'seq')), may hold values from -0.09375 to 0.09375
Outputs:
- mixed_out: bfloat16 [8192, 4096], P(('seq', 'tp'))
Inputs may be any that keep to these rules, and one draw needn't show every extreme that they name: poles lie strictly between 0 and 1.
All inputs are finite; a program needn't handle non-finite values.
Results may differ from a plain program's by a relative error of at most 0.0121.
Values may be sent and summed in bfloat16 or wider, within the bound.
No kernel may reach another device: no remote copies, remote signals or barrier semaphores. Data moves between devices by JAX's collectives and lax.ppermute only.
A program may use at most 192 MiB of HBM per device.

v0:
```python
import jax
import jax.numpy as jnp
from jax import lax
from jax.sharding import PartitionSpec as P

BLOCK = 64


def passed_along(value, axis, steps):
    count = lax.axis_size(axis)
    initial, last = (max(0, -steps), min(count, count - steps))
    return lax.ppermute(value, axis, [(source, source + steps) for source in range(initial, last)])


def carried_in(value, axis, join, neutral):
    count, mine = (lax.axis_size(axis), lax.axis_index(axis))
    pieces = jax.tree.map(lambda part: lax.all_gather(part, axis), value)
    running = jax.tree.map(
        lambda part, zero: jnp.full_like(part, 0) + jnp.asarray(zero, part.dtype), value, neutral
    )

    def step(position, running):
        longer = join(running, jax.tree.map(lambda part: part[position], pieces))
        return jax.tree.map(lambda new, old: jnp.where(position < mine, new, old), longer, running)

    return lax.fori_loop(0, count - 1, step, running)


def combine_states(earlier, later):
    return (earlier[0] * later[0], later[0] * earlier[1] + later[1])


def body(tokens, table, short_kernel, poles, residues, skip, out_weight):
    count = tokens.shape[0]
    vocab = table.shape[0]
    chans = table.shape[2]
    highest = lax.Precision.HIGHEST
    onehot = (tokens[:, None] == jnp.arange(vocab, dtype=jnp.int32)[None, :]).astype(jnp.bfloat16)
    streams = jnp.dot(onehot, table.reshape(vocab, 3 * chans), preferred_element_type=jnp.float32)
    streams = streams.astype(jnp.bfloat16).reshape(count, 3, chans)
    earlier = passed_along(streams[count - 2 :], "seq", 1)
    extended = jnp.concatenate([earlier, streams], axis=0).astype(jnp.float32)
    mixed = (
        short_kernel[0] * extended[2:]
        + short_kernel[1] * extended[1:-1]
        + short_kernel[2] * extended[:-2]
    )
    query = mixed[:, 0]
    drive = mixed[:, 1] * mixed[:, 2]
    width = BLOCK
    nblocks = count // width
    log_pole = jnp.log(poles)
    lags = jnp.arange(width, dtype=jnp.float32)
    blocks = drive.reshape(nblocks, width, chans)
    tails = jnp.exp((width - 1.0 - lags)[None, None, :] * log_pole[:, :, None])
    block_end = jnp.einsum("nct,btc->bnc", tails, blocks, precision=highest)
    step_decay = jnp.exp(width * log_pole)

    def advance(running, ends):
        return (step_decay * running + ends, running)

    zeros = jnp.zeros_like(poles)
    span_state, local_starts = lax.scan(advance, zeros, block_end)
    span_decay = jnp.exp(count * log_pole)
    incoming = carried_in(
        (span_decay, span_state), "seq", combine_states, (jnp.ones_like(poles), zeros)
    )[1]
    powers = jnp.exp(lags[None, None, :] * log_pole[:, :, None])
    kernel_taps = jnp.einsum("nc,nct->ct", residues, powers, precision=highest)
    offsets = jnp.arange(width)[:, None] - jnp.arange(width)[None, :]
    toeplitz = jnp.where(offsets[None] >= 0, kernel_taps[:, jnp.maximum(offsets, 0)], 0.0)
    inner = jnp.einsum("cts,bsc->btc", toeplitz, blocks, precision=highest)
    block_index = jnp.arange(nblocks, dtype=jnp.float32)
    starts = (
        local_starts + jnp.exp(block_index[:, None, None] * width * log_pole[None]) * incoming[None]
    )
    lead = residues[:, :, None] * jnp.exp((lags + 1.0)[None, None, :] * log_pole[:, :, None])
    carried = jnp.einsum("nct,bnc->btc", lead, starts, precision=highest)
    filtered = (inner + carried).reshape(count, chans)
    gated = (query * (filtered + skip * drive)).astype(jnp.bfloat16)
    weight_block = lax.all_gather(out_weight, "seq", axis=0, tiled=True)
    result = lax.psum_scatter(
        jnp.dot(gated, weight_block, preferred_element_type=jnp.float32).astype(jnp.bfloat16),
        "tp",
        scatter_dimension=0,
        tiled=True,
    )
    return result


def solution(mesh):
    placed = (
        P("seq"),
        P(None, None, "tp"),
        P(None, None, "tp"),
        P(None, "tp"),
        P(None, "tp"),
        P("tp"),
        P(("tp", "seq"), None),
    )
    return jax.shard_map(
        body, mesh=mesh, in_specs=placed, out_specs=P(("seq", "tp"), None), check_vma=False
    )
```

profile of v0, /device:TPU:1, one launch (start us, length us, event | category | flops | bytes accessed | tf_op | source)
XLA Modules:
  0.0 289.7 jit_solution(14951159318129547664)
XLA Ops:
  6.5 1.5 multiply_exponential_fusion
  8.1 3.2 %copy.16 = bf16[512,3,1024]{0,2,1:T(8,128)(2,1)S(1)} copy(bf16[512,3,1024]{2,0,1:T(8,128)(2,1)} %param.12) | data formatting | bytes 6291456 | tf_op args[1]
  11.4 2.1 convolution_convert_fusion.1
  14.2 4.9 %collective-permute-start = (bf16[2,3,1024]{2,1,0:T(4,128)(2,1)S(1)}, bf16[2,3,1024]{2,1,0:T(4,128)(2,1)S(1)}, u32[]{:S(2)}, u32[]{:S(2)}) collective-permute-start(bf16[2,3,1024]{2,1,0:T(4,128)(2,1)S(1)} %slice.35), channel_id=1, source_target_pairs={{0,4},{4,8},{8,12},{12,16},{16,20},{20,24},{24,28},{28,32},{32,36}... | collective-permute-start | bytes 36872 | tf_op jit(solution)/shard_map/ppermute | solution.py:12
  19.2 1.5 copy.17
  20.8 1.0 copy.20
  22.8 2.4 fusion.18
  25.2 1.0 copy.19
  26.2 1.5 copy.22
  27.7 15.7 %fusion.26 = f32[2,16,1024]{1,0,2:T(2,128)} fusion(f32[2,64,1024]{1,0,2:T(2,128)S(1)} %copy.22, f32[64]{0:T(128)S(1)} %iota_subtract_fusion, f32[16,1024]{0,1:T(8,128)} %copy.20), kind=kOutput, calls=%fused_computation.34 | convolution fusion | flops 26214400 | bytes 721152 | tf_op jit(solution)/shard_map/nct,btc->bnc/dot_general | solution.py:56
  43.4 1.4 copy.24
  44.8 1.4 while.27
  47.9 1.0 copy.25
  48.9 1.0 copy.35
  49.9 13.4 %multiply_reduce_fusion = f32[1024,64]{1,0:T(8,128)} fusion(f32[1024,16]{1,0:T(8,128)} %copy.35, f32[16,1024]{0,1:T(8,128)} %copy.20), kind=kLoop, calls=%fused_computation.11 | loop fusion | flops 3080192 | bytes 393216
  63.3 1.2 copy.34
  64.6 18.5 %gather_fusion = f32[4096,1024]{1,0:T(8,128)} fusion(f32[1024,64]{0,1:T(8,128)S(1)} %copy.34, s32[4096]{0:T(1024)S(1)} %broadcast_clamp_fusion), kind=kCustom, calls=%fused_computation | custom fusion | bytes 33570816 | tf_op jit(solution)/shard_map/gather | solution.py:71
  83.1 30.5 %copy.21 = f32[64,64,1024]{1,0,2:T(8,128)} copy(f32[64,64,1024]{2,1,0:T(8,128)} %bitcast.67) | data formatting | bytes 33554432 | tf_op jit(solution)/shard_map/gather | solution.py:71
  113.6 56.5 %fusion.1 = f32[1024,2,64]{2,1,0:T(2,128)} fusion(f32[2,64,1024]{1,0,2:T(2,128)S(1)} %copy.22, f32[64,64,1024]{1,0,2:T(8,128)} %copy.21, pred[64,64]{1,0:T(8,128)(4,1)S(1)} %subtract_compare_fusion), kind=kOutput, calls=%fused_computation.6 | convolution fusion | flops 104857600 | bytes 17829888 | tf_op jit(solution)/shard_map/cts,bsc->btc/dot_general | solution.py:72
  170.1 2.5 all-gather.10.cloned.1.call-done
  172.6 59.1 %while.28 = (s32[]{:T(128)}, f32[16,1024]{1,0:T(8,128)S(1)}, s32[]{:T(128)}, f32[64,16,1024]{2,1,0:T(8,128)}, f32[64,16,1024]{2,1,0:T(8,128)}, /*index=5*/s32[]{:T(128)}, s32[]{:T(128)}) while((s32[]{:T(128)}, f32[16,1024]{1,0:T(8,128)S(1)}, s32[]{:T(128)}, f32[64,16,1024]{2,1,0:T(8,128)}, f32[64,16,1024]{2,1,0:T(8,128)}, ...), condition=%wide.region_3.4_spmd.clone, body=%wide.region_2.3_spmd.clone.sunk | while | flops 65540 | bytes 262245 | solution.py:26
  173.5 0.9 fusion.45
  174.5 0.9 fusion.45
  175.4 0.9 fusion.45
  176.3 0.9 fusion.45
  177.3 0.9 fusion.45
  178.2 0.9 fusion.45
  179.2 0.9 fusion.45
  180.1 0.9 fusion.45
  181.0 0.9 fusion.45
  182.0 0.9 fusion.45
  182.9 0.9 fusion.45
  183.8 0.9 fusion.45
  184.8 0.9 fusion.45
  185.7 0.9 fusion.45
  186.7 0.9 fusion.45
  187.6 0.9 fusion.45
  188.5 0.9 fusion.45
  189.5 0.9 fusion.45
  190.4 0.9 fusion.45
  191.3 0.9 fusion.45
  192.3 0.9 fusion.45
  193.2 0.9 fusion.45
  194.2 0.9 fusion.45
  195.1 0.9 fusion.45
  196.0 0.9 fusion.45
  197.0 0.9 fusion.45
  198.8 0.9 fusion.45
  202.6 0.9 fusion.45
  208.2 0.9 fusion.45
  209.1 0.9 fusion.45
  217.6 0.9 fusion.45
  221.3 0.9 fusion.45
  223.2 0.9 fusion.45
  224.1 0.9 fusion.45
  226.9 1.0 fusion.45
  228.9 0.9 fusion.45
  229.8 1.0 fusion.45
  231.7 1.0 multiply_add_fusion
  233.3 13.1 %fusion.23 = f32[2,64,1024]{1,0,2:T(2,128)} fusion(f32[1024,2,64]{2,1,0:T(2,128)} %fusion.1, f32[2,16,1024]{1,0,2:T(2,128)S(1)} %copy.26, f32[64]{0:T(128)S(1)} %iota_add_fusion, f32[16,1024]{0,1:T(8,128)} %copy.25, f32[16,1024]{0,1:T(8,128)} %copy.20), kind=kOutput, calls=%fused_computation.33 | convolution fusion | flops 27394048 | bytes 1310976 | tf_op jit(solution)/shard_map/nct,bnc->btc/dot_general | solution.py:78
  246.3 1.5 copy.27
  248.0 7.8 %all-gather.6.cloned.1.call-done = bf16[1024,4096]{1,0:T(8,128)(2,1)} async-done(((bf16[16,4096]{1,0:T(8,128)(2,1)}), bf16[1024,4096]{1,0:T(8,128)(2,1)}) %all-gather.6.cloned.1.call-update) | async-done | bytes 8388624 | tf_op jit(solution)/shard_map/all_gather | solution.py:81
  255.8 5.7 %convolution_convert_fusion = bf16[128,4096]{1,0:T(8,128)(2,1)} fusion(bf16[1024,4096]{1,0:T(8,128)(2,1)} %all-gather.6.cloned.1.call-done, f32[128,3,1024]{0,2,1:T(8,128)S(1)} %fusion.18, f32[128,1024]{0,1:T(8,128)S(1)} %copy.28, f32[128,1,1024]{0,2,1:T(8,128)S(1)} %slice_multiply_fusion.3, f32[1024]{0:T(1024)S(1)} %copy-done.4), kind=kOutput, calls=%fused_computation.19 | convolution fusion | flops 1074790400 | bytes 11014144 | tf_op jit(solution)/shard_map/dot_general | solution.py:83
  261.5 21.7 %reduce-scatter.2.cloned.1.call-done = bf16[32,4096]{1,0:T(8,128)(2,1)} async-done(((bf16[128,4096]{1,0:T(8,128)(2,1)}), bf16[32,4096]{1,0:T(8,128)(2,1)}) %reduce-scatter.2.cloned.1.call-update) | async-done | bytes 262160 | tf_op jit(solution)/shard_map/reduce_scatter | solution.py:82
  (72 shorter events, 29.6 us)
Async XLA Ops:
  6.5 4.8 %copy-start.6 = (s32[128]{0:T(128)S(1)}, s32[128]{0:T(128)}, u32[]{:S(2)}) copy-start(s32[128]{0:T(128)} %param.11) | copy-start | bytes 1540
  6.5 163.6 %all-gather.8.cloned.1.call-start = ((), (), s32[]{:S(2)}) async-start(), calls=%async_computation.3 | async-start | bytes 4259840 | tf_op jit(solution)/shard_map/all_gather | solution.py:17
  8.1 12.7 %copy-start.1 = (f32[16,1024]{1,0:T(8,128)}, f32[16,1024]{1,0:T(8,128)S(1)}, u32[]{:S(2)}) copy-start(f32[16,1024]{1,0:T(8,128)S(1)} %get-tuple-element.198) | copy-start | bytes 196612
  8.1 11.1 %copy-start.5 = (f32[3,3,1024]{2,1,0:T(4,128)S(1)}, f32[3,3,1024]{2,1,0:T(4,128)}, u32[]{:S(2)}) copy-start(f32[3,3,1024]{2,1,0:T(4,128)} %param.13) | copy-start | bytes 110596
  8.1 164.5 %all-gather.10.cloned.1.call-start = ((), (), s32[]{:S(2)}) async-start(), calls=%async_computation.4 | async-start | bytes 4259840 | tf_op jit(solution)/shard_map/all_gather | solution.py:17
  14.2 7.5 %collective-permute-start = (bf16[2,3,1024]{2,1,0:T(4,128)(2,1)S(1)}, bf16[2,3,1024]{2,1,0:T(4,128)(2,1)S(1)}, u32[]{:S(2)}, u32[]{:S(2)}) collective-permute-start(bf16[2,3,1024]{2,1,0:T(4,128)(2,1)S(1)} %slice.35), channel_id=1, source_target_pairs={{0,4},{4,8},{8,12},{12,16},{16,20},{20,24},{24,28},{28,32},{32,36}... | collective-permute-start | bytes 36872 | tf_op jit(solution)/shard_map/ppermute | solution.py:12
  27.7 20.2 %copy-start.3 = (f32[16,1024]{1,0:T(8,128)S(1)}, f32[16,1024]{1,0:T(8,128)}, u32[]{:S(2)}) copy-start(f32[16,1024]{1,0:T(8,128)} %param.15) | copy-start | bytes 196612
  46.2 0.6 copy-start
  46.8 208.9 %all-gather.6.cloned.1.call-start = ((), (), s32[]{:S(2)}) async-start(), calls=%async_computation.1 | async-start | bytes 8519680 | tf_op jit(solution)/shard_map/all_gather | solution.py:81
  47.6 235.6 %reduce-scatter.2.cloned.1.call-start = ((), (), s32[]{:S(2)}) async-start(), calls=%async_computation.2 | async-start | bytes 1310720 | tf_op jit(solution)/shard_map/reduce_scatter | solution.py:82
  113.6 118.1 %copy-start.2 = (f32[16,1024]{1,0:T(8,128)S(1)}, f32[16,1024]{1,0:T(8,128)}, u32[]{:S(2)}) copy-start(f32[16,1024]{1,0:T(8,128)} %copy-done.1) | copy-start | bytes 196612
  233.3 22.5 %copy-start.4 = (f32[1024]{0:T(1024)S(1)}, f32[1024]{0:T(1024)}, u32[]{:S(2)}) copy-start(f32[1024]{0:T(1024)} %param.16) | copy-start | bytes 12292
Sparse Core Ops, SparseCore 0:
  10.1 83.2 all-gather.7
  96.2 76.3 all-gather.9
  175.4 80.3 all-gather.5
  261.6 21.5 reduce-scatter.1
where the time goes:
time: 294 us; the launch traced here: 290 us
  matrix products  93.1 us (32%)
  other arithmetic  78 us (27%)
  local copies, waits for them, and re-layouts  66 us (22%)
  waiting for transfers between devices  32.6 us (11%)
  between operations  13.4 us (5%)
  starting transfers between devices  5.24 us (2%)
    select_n x63, other arithmetic, step(): jnp.where(position < mine, new, old)  57.8 us
    dot_general x1, matrix products, body(): inner = jnp.einsum('cts,bsc->btc', toeplitz, blocks, precision=highest)  56.5 us
    gather x2, local copies, waits for them, and re-layouts, body(): kernel_taps[:, jnp.maximum(offsets, 0)]  49 us
    reduce_scatter x1, waiting for transfers between devices, body(): lax.psum_scatter(jnp.dot(gated, weight_block, preferred_element_type=jnp....  21.7 us
    dot_general x1, matrix products, body(): block_end = jnp.einsum('nct,btc->bnc', tails, blocks, precision=highest)  15.7 us
    unnamed x3, other arithmetic  13.4 us
    dot_general x1, matrix products, body(): carried = jnp.einsum('nct,bnc->btc', lead, starts, precision=highest)  13.1 us
    all_gather x1, waiting for transfers between devices, body(): weight_block = lax.all_gather(out_weight, 'seq', axis=0, tiled=True)  7.75 us
  transfers between devices with their start and end apart: 5, of which 3 were waited for; matrix products, arithmetic and copies ran while one was open for 79% of the time, Pallas kernels for 0%

commit v1 on v0

v1 whole, which is shorter than its diff:
```python
import functools

import jax
import jax.numpy as jnp
from jax import lax
from jax.experimental import pallas as pl
from jax.experimental.pallas import tpu as pltpu
from jax.sharding import PartitionSpec as P

F32 = jnp.float32
BF16 = jnp.bfloat16
TOK = 128
HALF = 512
MODES = 16
STEP = 136
VMEM = 48 * 1024 * 1024


def segment_rows(t):
    return pl.ds(t, 8, stride=STEP)


def spread(scratch, value, first):
    for q in range(4):
        scratch[pl.ds(first + q, MODES, stride=8), :] = value[:, q * 128 : (q + 1) * 128]


def squared(value, times):
    for _ in range(times):
        value = value * value
    return value


def scan_kernel(
    info, own, other, before_a, before_b, table, taps, poles, residues, skip,
    query_out, base_out, states_out, first_out,
    streams, drive_scr, filt_scr, pole_scr, res_scr, state_scr,
):
    core, chip = info[0], info[1]
    ids_own, ids_other = own[...], other[...]
    first = jnp.where(core == 0, ids_own, ids_other)
    second = jnp.where(core == 0, ids_other, ids_own)
    before = jnp.where(chip == 0, -1, before_a[...] + before_b[...])
    hots = []
    for ids, low in ((before, TOK - 16), (first, 0), (second, 0)):
        column = jnp.transpose(jnp.broadcast_to(ids, (128, TOK)))[low:]
        parts = [
            (column == lax.broadcasted_iota(jnp.int32, column.shape, 1) + 128 * k).astype(F32)
            for k in range(4)
        ]
        hots.append(jnp.concatenate(parts, axis=1))
    hot = jnp.concatenate(hots, axis=0).astype(BF16)
    for j in range(3):
        streams[j] = jnp.dot(hot, table[j], preferred_element_type=F32)

    def mixed(j):
        return (
            taps[0, j : j + 1] * streams[j, 16 : 16 + 2 * TOK]
            + taps[1, j : j + 1] * streams[j, 15 : 15 + 2 * TOK]
            + taps[2, j : j + 1] * streams[j, 14 : 14 + 2 * TOK]
        )

    drive = mixed(1) * mixed(2)
    for s in range(2):
        for q in range(4):
            row = (s * 4 + q) * STEP
            drive_scr[row : row + TOK] = drive[s * TOK : (s + 1) * TOK, q * 128 : (q + 1) * 128]
    for first_row in (0, 4):
        spread(pole_scr, poles[...], first_row)
        spread(res_scr, residues[...], first_row)
    pole = [pole_scr[n * 8 : (n + 1) * 8] for n in range(MODES)]
    res = [res_scr[n * 8 : (n + 1) * 8] for n in range(MODES)]

    def advance(t, modes):
        value = drive_scr[segment_rows(t), :]
        modes = tuple(pole[n] * modes[n] + value for n in range(MODES))
        terms = [res[n] * modes[n] for n in range(MODES)]
        while len(terms) > 1:
            terms = [a + b for a, b in zip(terms[::2], terms[1::2])]
        filt_scr[segment_rows(t), :] = terms[0]
        return modes

    modes = lax.fori_loop(0, TOK, advance, (jnp.zeros((8, 128), F32),) * MODES, unroll=4)
    for n in range(MODES):
        state_scr[n * 8 : (n + 1) * 8] = modes[n]
    query = mixed(0)
    query_out[...] = query
    ends = []
    for q in range(4):
        lanes = slice(q * 128, (q + 1) * 128)
        one = state_scr[pl.ds(q, MODES, stride=8), :]
        two = state_scr[pl.ds(4 + q, MODES, stride=8), :]
        first_out[q * MODES : (q + 1) * MODES] = one
        ends.append((squared(poles[:, lanes], 7) * one + two).astype(BF16))
        for s in range(2):
            rows = slice(s * TOK, (s + 1) * TOK)
            row = (s * 4 + q) * STEP
            filtered = filt_scr[row : row + TOK] + skip[:, lanes] * drive[rows, lanes]
            base_out[rows, lanes] = query[rows, lanes] * filtered
    end = jnp.concatenate(ends, axis=0)
    for chip_to in range(states_out.shape[0]):
        states_out[chip_to] = end


def gate_kernel(
    info, states, first, poles, residues, query, base, keep_out, send_out, coef_scr, pole_scr, corr_scr, gated_scr
):
    core, chip, place, groups = info[0], info[1], info[2], keep_out.shape[0] // 32
    flat = [poles[:, q * 128 : (q + 1) * 128] for q in range(4)]
    pole = jnp.concatenate(flat, axis=0)
    lead = jnp.concatenate([residues[:, q * 128 : (q + 1) * 128] for q in range(4)], axis=0) * pole
    half = squared(pole, 7)
    whole = half * half

    def join(source, running):
        return whole * running + states[source].astype(F32)

    incoming = lax.fori_loop(0, chip, join, jnp.zeros((4 * MODES, 128), F32))
    coefs = (lead * incoming, lead * (half * incoming + first[...]))
    for s in range(2):
        for q in range(4):
            coef_scr[pl.ds(s * 4 + q, MODES, stride=8), :] = coefs[s][q * MODES : (q + 1) * MODES]
        spread(pole_scr, poles[...], s * 4)
    mode_pole = [pole_scr[n * 8 : (n + 1) * 8] for n in range(MODES)]
    start = tuple(coef_scr[n * 8 : (n + 1) * 8] for n in range(MODES))

    def decay(t, terms):
        total = list(terms)
        while len(total) > 1:
            total = [a + b for a, b in zip(total[::2], total[1::2])]
        corr_scr[segment_rows(t), :] = total[0]
        return tuple(mode_pole[n] * terms[n] for n in range(MODES))

    lax.fori_loop(0, TOK, decay, start, unroll=4)
    for s in range(2):
        for q in range(4):
            rows, lanes = slice(s * TOK, (s + 1) * TOK), slice(q * 128, (q + 1) * 128)
            row = (s * 4 + q) * STEP
            gated_scr[rows, lanes] = base[rows, lanes] + query[rows, lanes] * corr_scr[row : row + TOK]
    for d in range(groups):
        spot = lax.rem(place + d, groups) * 32
        for out, whose in ((keep_out, core), (send_out, 1 - core)):
            rows = pl.ds(pl.multiple_of(whose * TOK + spot, 32), 32)
            out[d * 32 : (d + 1) * 32] = gated_scr[rows, :].astype(BF16)


def project_kernel(info, keep, came, weight, *outs):
    core = info[0]
    mine = weight[pl.ds(pl.multiple_of(core * HALF, HALF), HALF), :]
    theirs = weight[pl.ds(pl.multiple_of((1 - core) * HALF, HALF), HALF), :]
    total = jnp.dot(keep[...], mine, preferred_element_type=F32) + jnp.dot(
        came[...], theirs, preferred_element_type=F32
    )
    for d, out in enumerate(outs):
        out[...] = total[d * 32 : (d + 1) * 32].astype(BF16)


def whole_block(shape):
    return pl.BlockSpec(shape, lambda i, info: (0,) * len(shape))


def core_block(shape):
    return pl.BlockSpec(shape, lambda i, info: (0,) * (len(shape) - 1) + (info[0],))


def call(kernel, name, info, args, in_specs, out_shape, out_specs, scratch=(), grid=1, flops=0, moved=0):
    return pl.pallas_call(
        kernel,
        grid_spec=pltpu.PrefetchScalarGridSpec(
            num_scalar_prefetch=1, grid=(grid,), in_specs=in_specs, out_specs=out_specs, scratch_shapes=scratch
        ),
        out_shape=out_shape,
        compiler_params=pltpu.CompilerParams(vmem_limit_bytes=VMEM),
        cost_estimate=pl.CostEstimate(flops=flops, bytes_accessed=moved, transcendentals=0),
        name=name,
    )(info, *args)


def body(tokens, table, short_kernel, poles, residues, skip, out_weight):
    n_seq, n_tp = lax.axis_size("seq"), lax.axis_size("tp")
    chips = n_seq // 2
    vocab, width = table.shape[0], out_weight.shape[1]
    index = lax.axis_index("seq")
    info = jnp.stack([index % 2, index // 2, lax.axis_index("tp")]).astype(jnp.int32)
    swap = [(i, i ^ 1) for i in range(n_seq)]
    weight = lax.all_gather(out_weight, "seq", axis=0, tiled=True)

    ids = tokens.reshape(1, TOK)
    other = lax.ppermute(ids, "seq", swap)
    before_a = lax.ppermute(ids, "seq", [(2 * p + 1, 2 * p + 2) for p in range(chips - 1)])
    before_b = lax.ppermute(ids, "seq", [(2 * p + 1, 2 * p + 3) for p in range(chips - 1)])
    ids_block = whole_block((1, TOK))
    tok_block = whole_block((2 * TOK, HALF))
    query, base, states, first = call(
        scan_kernel, "scan", info,
        (ids, other, before_a, before_b, jnp.transpose(table, (1, 0, 2)), short_kernel, poles, residues, skip.reshape(1, -1)),
        [ids_block] * 4
        + [core_block((3, vocab, HALF)), core_block((3, 3, HALF)), core_block((MODES, HALF)), core_block((MODES, HALF)), core_block((1, HALF))],
        (
            jax.ShapeDtypeStruct((2 * TOK, HALF), F32),
            jax.ShapeDtypeStruct((2 * TOK, HALF), F32),
            jax.ShapeDtypeStruct((chips, 4 * MODES, 128), BF16),
            jax.ShapeDtypeStruct((4 * MODES, 128), F32),
        ),
        (tok_block, tok_block, whole_block((chips, 4 * MODES, 128)), whole_block((4 * MODES, 128))),
        scratch=(
            pltpu.VMEM((3, 2 * TOK + 16, HALF), F32),
            pltpu.VMEM((8 * STEP, 128), F32),
            pltpu.VMEM((8 * STEP, 128), F32),
            pltpu.VMEM((MODES * 8, 128), F32),
            pltpu.VMEM((MODES * 8, 128), F32),
            pltpu.VMEM((MODES * 8, 128), F32),
        ),
        flops=600_000_000, moved=4_000_000,
    )
    states = lax.all_to_all(
        states, "seq", 0, 0, axis_index_groups=[[2 * p + c for p in range(chips)] for c in range(2)]
    )
    keep, send = call(
        gate_kernel, "gate", info, (states, first, poles, residues, query, base),
        [whole_block((chips, 4 * MODES, 128)), whole_block((4 * MODES, 128)), core_block((MODES, HALF)), core_block((MODES, HALF)), tok_block, tok_block],
        (jax.ShapeDtypeStruct((TOK, HALF), BF16),) * 2,
        (whole_block((TOK, HALF)),) * 2,
        scratch=(
            pltpu.VMEM((MODES * 8, 128), F32),
            pltpu.VMEM((MODES * 8, 128), F32),
            pltpu.VMEM((8 * STEP, 128), F32),
            pltpu.VMEM((2 * TOK, HALF), F32),
        ),
        flops=20_000_000, moved=2_000_000,
    )
    came = lax.ppermute(send, "seq", swap)
    tile = 512
    rows = TOK // n_tp
    parts = call(
        project_kernel, "project", info, (keep, came, weight),
        [whole_block((TOK, HALF)), whole_block((TOK, HALF)), pl.BlockSpec((2 * HALF, tile), lambda i, info: (0, i))],
        (jax.ShapeDtypeStruct((rows, width), BF16),) * n_tp,
        (pl.BlockSpec((rows, tile), lambda i, info: (0, i)),) * n_tp,
        grid=width // tile, flops=2 * TOK * 2 * HALF * width, moved=2 * HALF * width * 2,
    )
    total = parts[0].astype(F32)
    for d in range(1, n_tp):
        total = total + lax.ppermute(parts[d], "tp", [(x, (x + d) % n_tp) for x in range(n_tp)]).astype(F32)
    return total.astype(BF16)


def solution(mesh):
    placed = (
        P("seq"),
        P(None, None, "tp"),
        P(None, None, "tp"),
        P(None, "tp"),
        P(None, "tp"),
        P("tp"),
        P(("tp", "seq"), None),
    )
    return jax.shard_map(
        body, mesh=mesh, in_specs=placed, out_specs=P(("seq", "tp"), None), check_vma=False
    )
```

time: 294 us -> 131 us (0.45); the launches traced: 290 us -> 130 us
  matrix products: 93.1 us -> 0 us
  other arithmetic: 78 us -> 0.91 us
  local copies, waits for them, and re-layouts: 66 us -> 5.71 us
  blocking collectives: 0 us -> 29.2 us
  waiting for transfers between devices: 32.6 us -> 55.5 us
  Pallas kernels: 0 us -> 11.8 us
  starting transfers between devices: 5.24 us -> 13.5 us
    dot_general x5 -> x0, matrix products: 93.1 us -> none  [the longest x1 56.5 us: body(): inner = jnp.einsum('cts,bsc->btc', toeplitz, blocks, precision=highest)]
    select_n x63 -> x0, other arithmetic: 57.8 us -> none  [step(): jnp.where(position < mine, new, old)]
    gather x2 -> x0, local copies, waits for them, and re-layouts: 49 us -> none  [body(): kernel_taps[:, jnp.maximum(offsets, 0)]]
    all_gather x3 -> x1, waiting for transfers between devices: 10.2 us -> 42 us  [body(): weight = lax.all_gather(out_weight, 'seq', axis=0, tiled=True)]
    all_to_all x0 -> x1, blocking collectives: none -> 29.2 us  [body(): lax.all_to_all(states, 'seq', 0, 0, axis_index_groups=[[2 * p + c for p i...]
    reduce_scatter x1 -> x0, waiting for transfers between devices: 21.7 us -> none  [body(): lax.psum_scatter(jnp.dot(gated, weight_block, preferred_element_type=jnp....]
    unnamed x3 -> x0, other arithmetic: 13.4 us -> none
    ppermute x1 -> x7, waiting for transfers between devices: 0.01 us -> 12.7 us  [the longest x3 10.6 us: body(): lax.ppermute(parts[d], 'tp', [(x, (x + d) % n_tp) for x in range(n_tp)])]
  transfers between devices with their start and end apart: 5 -> 8, of which waited for: 3 -> 5; matrix products, arithmetic and copies ran while one was open for 79% -> 0% of each run, Pallas kernels for 0% -> 3%
where the time goes in v1:
time: 131 us; the launch traced here: 130 us
  waiting for transfers between devices  55.5 us (42%)
  blocking collectives  29.2 us (22%)
  starting transfers between devices  13.5 us (10%)
  between operations  13.5 us (10%)
  Pallas kernels  11.8 us (9%)
  local copies, waits for them, and re-layouts  5.71 us (4%)
    all_gather x1, waiting for transfers between devices, body(): weight = lax.all_gather(out_weight, 'seq', axis=0, tiled=True)  42 us
    all_to_all x1, blocking collectives, body(): lax.all_to_all(states, 'seq', 0, 0, axis_index_groups=[[2 * p + c for p i...  29.2 us
    pallas_call x3, Pallas kernels, call(): pl.pallas_call(kernel, grid_spec=pltpu.PrefetchScalarGridSpec(num_scalar_...  11.8 us
    ppermute x3, waiting for transfers between devices, body(): lax.ppermute(parts[d], 'tp', [(x, (x + d) % n_tp) for x in range(n_tp)])  10.6 us
    unnamed x12, local copies, waits for them, and re-layouts  5.71 us
    ppermute x3, starting transfers between devices, body(): lax.ppermute(parts[d], 'tp', [(x, (x + d) % n_tp) for x in range(n_tp)])  4.85 us
    ppermute x1, starting transfers between devices, body(): lax.ppermute(ids, 'seq', [(2 * p + 1, 2 * p + 3) for p in range(chips - 1)])  3.54 us
    ppermute x1, starting transfers between devices, body(): other = lax.ppermute(ids, 'seq', swap)  3.33 us
  transfers between devices with their start and end apart: 8, of which 5 were waited for; matrix products, arithmetic and copies ran while one was open for 0% of the time, Pallas kernels for 3%

profile of v1, /device:TPU:1, one launch (start us, length us, event | category | flops | bytes accessed | tf_op | source)
XLA Modules:
  0.0 130.1 jit_solution(8977588069414269956)
XLA Ops:
  6.5 0.0 all-gather.2.cloned.1.call-start
  6.5 0.7 all-gather.2.cloned.1.call-update
  7.3 3.3 %collective-permute-start = (s32[1,128]{1,0:T(1,128)}, s32[1,128]{1,0:T(1,128)S(1)}, u32[]{:S(2)}, u32[]{:S(2)}) collective-permute-start(s32[1,128]{1,0:T(1,128)} %bitcast.8), channel_id=1, source_target_pairs={{0,4},{4,0},{8,12},{12,8},{16,20},{20,16},{24,28},{28,24},{32,36},... | collective-permute-start | bytes 1544 | tf_op jit(solution)/shard_map/ppermute | solution.py:189
  10.6 1.7 %collective-permute-start.1 = (s32[1,128]{1,0:T(1,128)}, s32[1,128]{1,0:T(1,128)S(1)}, u32[]{:S(2)}, u32[]{:S(2)}) collective-permute-start(s32[1,128]{1,0:T(1,128)} %bitcast.9), channel_id=1, source_target_pairs={{4,8},{12,16},{20,24},{28,32},{36,40},{44,48},{52,56},{60,64},{68,... | collective-permute-start | bytes 1544 | tf_op jit(solution)/shard_map/ppermute | solution.py:190
  12.3 3.5 %collective-permute-start.2 = (s32[1,128]{1,0:T(1,128)}, s32[1,128]{1,0:T(1,128)S(1)}, u32[]{:S(2)}, u32[]{:S(2)}) collective-permute-start(s32[1,128]{1,0:T(1,128)} %bitcast.10), channel_id=1, source_target_pairs={{4,12},{12,20},{20,28},{28,36},{36,44},{44,52},{52,60},{60,68},{68... | collective-permute-start | bytes 1544 | tf_op jit(solution)/shard_map/ppermute | solution.py:191
  15.9 0.1 pad_add_fusion.info
  15.9 0.0 collective-permute-done.other
  16.0 0.0 collective-permute-done.1.before_a
  16.0 0.7 collective-permute-done.2.before_b
  16.7 0.0 copy-start
  16.7 1.9 %copy-done = bf16[512,3,1024]{2,0,1:T(8,128)(2,1)S(1)} copy-done((bf16[512,3,1024]{2,0,1:T(8,128)(2,1)S(1)}, bf16[512,3,1024]{2,0,1:T(8,128)(2,1)}, u32[]{:S(2)}) %copy-start) | copy-done | bytes 3145752
  18.6 0.0 copy-start.1
  18.6 0.8 copy-done.1
  19.4 0.0 copy-start.2
  19.4 0.8 copy-done.2
  20.3 0.0 copy-start.3
  20.3 0.8 copy-done.3
  21.1 0.0 copy-start.4
  21.1 0.7 copy-done.4
  21.7 0.0 copy-start.5
  21.7 0.7 copy-done.5
  22.4 3.2 %scan.1 = (f32[256,512]{1,0:T(8,128)S(1)}, f32[256,512]{1,0:T(8,128)S(1)}, bf16[32,64,128]{2,1,0:T(8,128)(2,1)S(1)}, f32[64,128]{1,0:T(8,128)S(1)}) custom-call(s32[3]{0:T(128)S(1)} %pad_add_fusion.info, s32[1,128]{1,0:T(1,128)S(1)} %bitcast.11, s32[1,128]{1,0:T(1,128)S(1)} %collective-permute-done.other, s32[1,128]{1,0:T(1,128)S(1)} %collective-permute-done.1.before_a, ...), custom_call_target="tpu_custom_call" | custom-call | flops 600000000 | bytes 4000000 | tf_op jit(solution)/shard_map/scan/pallas_call | solution.py:167
  25.6 29.2 %all_to_all.5.states = bf16[32,64,128]{2,1,0:T(8,128)(2,1)S(1)} all-to-all(bf16[32,64,128]{2,1,0:T(8,128)(2,1)S(1)} %get-tuple-element.15), channel_id=1, replica_groups={{0,8,16,24,32,40,48,56,64,72,80,88,96,104,112,120,128,136,144,152,160,1..., dimensions={0} | all-to-all | bytes 1048576 | tf_op jit(solution)/shard_map/all_to_all | solution.py:216
  54.8 1.3 %gate.1 = (bf16[128,512]{1,0:T(8,128)(2,1)S(1)}, bf16[128,512]{1,0:T(8,128)(2,1)S(1)}) custom-call(s32[3]{0:T(128)S(1)} %pad_add_fusion.info, bf16[32,64,128]{2,1,0:T(8,128)(2,1)S(1)} %all_to_all.5.states, f32[64,128]{1,0:T(8,128)S(1)} %get-tuple-element.16.first, f32[16,1024]{1,0:T(8,128)S(1)} %copy-done.1, f32[16,1024]{1,0:T(8,128)S(1)} %copy-done.2, ...), custom_call_target="tpu_custom_call" | custom-call | flops 20000000 | bytes 2000000 | tf_op jit(solution)/shard_map/gate/pallas_call | solution.py:167
  56.1 0.1 collective-permute-start.3
  56.2 1.3 %collective-permute-done.3.came = bf16[128,512]{1,0:T(8,128)(2,1)S(1)} collective-permute-done((bf16[128,512]{1,0:T(8,128)(2,1)S(1)}, bf16[128,512]{1,0:T(8,128)(2,1)S(1)}, u32[]{:S(2)}, u32[]{:S(2)}) %collective-permute-start.3) | collective-permute-done | bytes 131104 | tf_op jit(solution)/shard_map/ppermute | solution.py:232
  57.5 42.0 %all-gather.2.cloned.1.call-done.weight = bf16[1024,4096]{1,0:T(8,128)(2,1)} async-done(((bf16[16,4096]{1,0:T(8,128)(2,1)}), bf16[1024,4096]{1,0:T(8,128)(2,1)}) %all-gather.2.cloned.1.call-update) | async-done | bytes 8388624 | tf_op jit(solution)/shard_map/all_gather | solution.py:186
  99.6 7.3 %project.1 = (bf16[32,4096]{1,0:T(8,128)(2,1)S(1)}, bf16[32,4096]{1,0:T(8,128)(2,1)S(1)}, bf16[32,4096]{1,0:T(8,128)(2,1)S(1)}, bf16[32,4096]{1,0:T(8,128)(2,1)S(1)}) custom-call(s32[3]{0:T(128)S(1)} %pad_add_fusion.info, bf16[128,512]{1,0:T(8,128)(2,1)S(1)} %get-tuple-element.19.keep, bf16[128,512]{1,0:T(8,128)(2,1)S(1)} %collective-permute-done.3.came, ...), custom_call_target="tpu_custom_call" | custom-call | flops 1073741824 | bytes 8388608 | tf_op jit(solution)/shard_map/project/pallas_call | solution.py:167
  106.9 1.3 collective-permute-start.4
  108.2 2.4 %collective-permute-start.5 = (bf16[32,4096]{1,0:T(8,128)(2,1)S(1)}, bf16[32,4096]{1,0:T(8,128)(2,1)S(1)}, u32[]{:S(2)}, u32[]{:S(2)}) collective-permute-start(bf16[32,4096]{1,0:T(8,128)(2,1)S(1)} %get-tuple-element.23), channel_id=1, source_target_pairs={{0,2},{1,3},{2,0},{3,1},{4,6},{5,7},{6,4},{7,5},{8,10},{9,11},{10,... | collective-permute-start | bytes 786440 | tf_op jit(solution)/shard_map/ppermute | solution.py:244
  110.6 1.2 collective-permute-start.6
  111.8 4.1 %collective-permute-done.4 = bf16[32,4096]{1,0:T(8,128)(2,1)S(1)} collective-permute-done((bf16[32,4096]{1,0:T(8,128)(2,1)S(1)}, bf16[32,4096]{1,0:T(8,128)(2,1)S(1)}, u32[]{:S(2)}, u32[]{:S(2)}) %collective-permute-start.4) | collective-permute-done | bytes 262176 | tf_op jit(solution)/shard_map/ppermute | solution.py:244
  115.9 6.5 %collective-permute-done.5 = bf16[32,4096]{1,0:T(8,128)(2,1)S(1)} collective-permute-done((bf16[32,4096]{1,0:T(8,128)(2,1)S(1)}, bf16[32,4096]{1,0:T(8,128)(2,1)S(1)}, u32[]{:S(2)}, u32[]{:S(2)}) %collective-permute-start.5) | collective-permute-done | bytes 262176 | tf_op jit(solution)/shard_map/ppermute | solution.py:244
  122.4 0.0 collective-permute-done.6
  122.4 0.8 add_convert_fusion
Async XLA Ops:
  6.5 93.0 %all-gather.2.cloned.1.call-start = ((), (), s32[]{:S(2)}) async-start(), calls=%async_computation.1 | async-start | bytes 8519680 | tf_op jit(solution)/shard_map/all_gather | solution.py:186
  7.3 8.7 %collective-permute-start = (s32[1,128]{1,0:T(1,128)}, s32[1,128]{1,0:T(1,128)S(1)}, u32[]{:S(2)}, u32[]{:S(2)}) collective-permute-start(s32[1,128]{1,0:T(1,128)} %bitcast.8), channel_id=1, source_target_pairs={{0,4},{4,0},{8,12},{12,8},{16,20},{20,16},{24,28},{28,24},{32,36},... | collective-permute-start | bytes 1544 | tf_op jit(solution)/shard_map/ppermute | solution.py:189
  10.6 5.4 %collective-permute-start.1 = (s32[1,128]{1,0:T(1,128)}, s32[1,128]{1,0:T(1,128)S(1)}, u32[]{:S(2)}, u32[]{:S(2)}) collective-permute-start(s32[1,128]{1,0:T(1,128)} %bitcast.9), channel_id=1, source_target_pairs={{4,8},{12,16},{20,24},{28,32},{36,40},{44,48},{52,56},{60,64},{68,... | collective-permute-start | bytes 1544 | tf_op jit(solution)/shard_map/ppermute | solution.py:190
  12.3 4.4 %collective-permute-start.2 = (s32[1,128]{1,0:T(1,128)}, s32[1,128]{1,0:T(1,128)S(1)}, u32[]{:S(2)}, u32[]{:S(2)}) collective-permute-start(s32[1,128]{1,0:T(1,128)} %bitcast.10), channel_id=1, source_target_pairs={{4,12},{12,20},{20,28},{28,36},{36,44},{44,52},{52,60},{60,68},{68... | collective-permute-start | bytes 1544 | tf_op jit(solution)/shard_map/ppermute | solution.py:191
  16.7 1.9 %copy-start = (bf16[512,3,1024]{2,0,1:T(8,128)(2,1)S(1)}, bf16[512,3,1024]{2,0,1:T(8,128)(2,1)}, u32[]{:S(2)}) copy-start(bf16[512,3,1024]{2,0,1:T(8,128)(2,1)} %param.8) | copy-start | bytes 9437188
  18.6 0.8 copy-start.1
  19.4 0.8 copy-start.2
  20.3 0.8 copy-start.3
  21.1 0.7 copy-start.4
  21.7 0.7 copy-start.5
  56.1 1.4 %collective-permute-start.3 = (bf16[128,512]{1,0:T(8,128)(2,1)S(1)}, bf16[128,512]{1,0:T(8,128)(2,1)S(1)}, u32[]{:S(2)}, u32[]{:S(2)}) collective-permute-start(bf16[128,512]{1,0:T(8,128)(2,1)S(1)} %get-tuple-element.20), channel_id=1, source_target_pairs={{0,4},{4,0},{8,12},{12,8},{16,20},{20,16},{24,28},{28,24},{32,36},... | collective-permute-start | bytes 393224 | tf_op jit(solution)/shard_map/ppermute | solution.py:232
  106.9 8.9 %collective-permute-start.4 = (bf16[32,4096]{1,0:T(8,128)(2,1)S(1)}, bf16[32,4096]{1,0:T(8,128)(2,1)S(1)}, u32[]{:S(2)}, u32[]{:S(2)}) collective-permute-start(bf16[32,4096]{1,0:T(8,128)(2,1)S(1)} %get-tuple-element.22), channel_id=1, source_target_pairs={{0,1},{1,2},{2,3},{3,0},{4,5},{5,6},{6,7},{7,4},{8,9},{9,10},{10,1... | collective-permute-start | bytes 786440 | tf_op jit(solution)/shard_map/ppermute | solution.py:244
  108.2 14.2 %collective-permute-start.5 = (bf16[32,4096]{1,0:T(8,128)(2,1)S(1)}, bf16[32,4096]{1,0:T(8,128)(2,1)S(1)}, u32[]{:S(2)}, u32[]{:S(2)}) collective-permute-start(bf16[32,4096]{1,0:T(8,128)(2,1)S(1)} %get-tuple-element.23), channel_id=1, source_target_pairs={{0,2},{1,3},{2,0},{3,1},{4,6},{5,7},{6,4},{7,5},{8,10},{9,11},{10,... | collective-permute-start | bytes 786440 | tf_op jit(solution)/shard_map/ppermute | solution.py:244
  110.6 11.8 %collective-permute-start.6 = (bf16[32,4096]{1,0:T(8,128)(2,1)S(1)}, bf16[32,4096]{1,0:T(8,128)(2,1)S(1)}, u32[]{:S(2)}, u32[]{:S(2)}) collective-permute-start(bf16[32,4096]{1,0:T(8,128)(2,1)S(1)} %get-tuple-element.24), channel_id=1, source_target_pairs={{0,3},{1,0},{2,1},{3,2},{4,7},{5,4},{6,5},{7,6},{8,11},{9,8},{10,9... | collective-permute-start | bytes 786440 | tf_op jit(solution)/shard_map/ppermute | solution.py:244
Sparse Core Ops, SparseCore 0:
  10.1 89.3 all-gather.1

commit v2 on v1

v2 whole, which is shorter than its diff:
```python
import functools

import jax
import jax.numpy as jnp
from jax import lax
from jax.experimental import pallas as pl
from jax.experimental.pallas import tpu as pltpu
from jax.sharding import PartitionSpec as P

F32 = jnp.float32
BF16 = jnp.bfloat16
TOK = 128
HALF = 512
MODES = 16
STEP = 136
VMEM = 62 * 1024 * 1024
NZ = 8
ALONG = (0, -1, 1, -2, 2, -3, 3)


def segment_rows(t):
    return pl.ds(t, 8, stride=STEP)


def spread(scratch, value, first):
    for q in range(4):
        scratch[pl.ds(first + q, MODES, stride=8), :] = value[:, q * 128 : (q + 1) * 128]


def squared(value, times):
    for _ in range(times):
        value = value * value
    return value


def scan_kernel(
    info, own, other, passed, table, taps, poles, residues, skip,
    query_out, base_out, states_out, first_out,
    streams, drive_scr, filt_scr, pole_scr, res_scr, state_scr,
):
    core, chip = info[0], info[1]
    ids_own, ids_other = own[...], other[0:1]
    first = jnp.where(core == 0, ids_own, ids_other)
    second = jnp.where(core == 0, ids_other, ids_own)
    before = jnp.where(chip == 0, -1, jnp.where(core == 0, passed[...], other[1:2]))
    hots = []
    for ids, low in ((before, TOK - 16), (first, 0), (second, 0)):
        column = jnp.transpose(jnp.broadcast_to(ids, (128, TOK)))[low:]
        parts = [
            (column == lax.broadcasted_iota(jnp.int32, column.shape, 1) + 128 * k).astype(F32)
            for k in range(4)
        ]
        hots.append(jnp.concatenate(parts, axis=1))
    hot = jnp.concatenate(hots, axis=0).astype(BF16)
    for j in range(3):
        streams[j] = jnp.dot(hot, table[j], preferred_element_type=F32)

    def mixed(j):
        return (
            taps[0, j : j + 1] * streams[j, 16 : 16 + 2 * TOK]
            + taps[1, j : j + 1] * streams[j, 15 : 15 + 2 * TOK]
            + taps[2, j : j + 1] * streams[j, 14 : 14 + 2 * TOK]
        )

    drive = mixed(1) * mixed(2)
    for s in range(2):
        for q in range(4):
            row = (s * 4 + q) * STEP
            drive_scr[row : row + TOK] = drive[s * TOK : (s + 1) * TOK, q * 128 : (q + 1) * 128]
    for first_row in (0, 4):
        spread(pole_scr, poles[...], first_row)
        spread(res_scr, residues[...], first_row)
    pole = [pole_scr[n * 8 : (n + 1) * 8] for n in range(MODES)]
    res = [res_scr[n * 8 : (n + 1) * 8] for n in range(MODES)]

    def advance(t, modes):
        value = drive_scr[segment_rows(t), :]
        modes = tuple(pole[n] * modes[n] + value for n in range(MODES))
        terms = [res[n] * modes[n] for n in range(MODES)]
        while len(terms) > 1:
            terms = [a + b for a, b in zip(terms[::2], terms[1::2])]
        filt_scr[segment_rows(t), :] = terms[0]
        return modes

    modes = lax.fori_loop(0, TOK, advance, (jnp.zeros((8, 128), F32),) * MODES, unroll=4)
    for n in range(MODES):
        state_scr[n * 8 : (n + 1) * 8] = modes[n]
    query = mixed(0)
    query_out[...] = query
    ends = []
    for q in range(4):
        lanes = slice(q * 128, (q + 1) * 128)
        rows = slice(q * MODES, (q + 1) * MODES)
        one = state_scr[pl.ds(q, MODES, stride=8), :]
        two = state_scr[pl.ds(4 + q, MODES, stride=8), :]
        half = squared(poles[:, lanes], 7)
        first_out[rows] = one
        ends.append((half * one + two).astype(BF16))
        for s in range(2):
            rows = slice(s * TOK, (s + 1) * TOK)
            row = (s * 4 + q) * STEP
            filtered = filt_scr[row : row + TOK] + skip[:, lanes] * drive[rows, lanes]
            base_out[rows, lanes] = query[rows, lanes] * filtered
    end = jnp.concatenate(ends, axis=0)
    for chip_to in range(states_out.shape[0]):
        states_out[chip_to] = end


def gate_kernel(
    groups, info, states, first, poles, residues, query, base, gated_out, coef_scr, pole_scr, corr_scr, gated_scr
):
    place, each = info[2], TOK // groups
    pole = jnp.concatenate([poles[:, q * 128 : (q + 1) * 128] for q in range(4)], axis=0)
    lead = jnp.concatenate([residues[:, q * 128 : (q + 1) * 128] for q in range(4)], axis=0) * pole
    half = squared(pole, 7)
    whole = half * half

    def join(source, running):
        return whole * running + states[source].astype(F32)

    incoming = lax.fori_loop(0, info[1], join, jnp.zeros((4 * MODES, 128), F32))
    coefs = (lead * incoming, lead * (half * incoming + first[...]))
    for s in range(2):
        for q in range(4):
            coef_scr[pl.ds(s * 4 + q, MODES, stride=8), :] = coefs[s][q * MODES : (q + 1) * MODES]
        spread(pole_scr, poles[...], s * 4)
    mode_pole = [pole_scr[n * 8 : (n + 1) * 8] for n in range(MODES)]
    start = tuple(coef_scr[n * 8 : (n + 1) * 8] for n in range(MODES))

    def decay(t, terms):
        total = list(terms)
        while len(total) > 1:
            total = [a + b for a, b in zip(total[::2], total[1::2])]
        corr_scr[segment_rows(t), :] = total[0]
        return tuple(mode_pole[n] * terms[n] for n in range(MODES))

    lax.fori_loop(0, TOK, decay, start, unroll=4)
    for s in range(2):
        for q in range(4):
            rows, lanes = slice(s * TOK, (s + 1) * TOK), slice(q * 128, (q + 1) * 128)
            row = (s * 4 + q) * STEP
            gated_scr[rows, lanes] = base[rows, lanes] + query[rows, lanes] * corr_scr[row : row + TOK]
    for owner in range(2):
        for d in range(groups):
            spot = pl.ds(pl.multiple_of(owner * TOK + lax.rem(place + d, groups) * each, each), each)
            row = owner * TOK + d * each
            gated_out[row : row + each] = gated_scr[spot, :].astype(BF16)


def place_kernel(info, *refs):
    column, blocks, last, outs = info[4], refs[:7], refs[7:9], refs[9:]
    for block, dz in zip(blocks, ALONG):
        rows = pl.ds(pl.multiple_of(lax.rem(column + dz + NZ, NZ) * 32, 32), 32)
        for k, out in enumerate(outs):
            cols = out.shape[1]
            out[rows, :] = block[:, k * cols : (k + 1) * cols]
    rows = pl.ds(pl.multiple_of(lax.rem(column + NZ // 2, NZ) * 32, 32), 32)
    for block, out in zip(last, outs):
        out[rows, :] = block[...]


def project_kernel(rows_of, info, ours, theirs, *refs):
    core, row = info[0], info[3]
    weights, outs, full = refs[:4], refs[4:-1], refs[-1]
    mine = pl.ds(pl.multiple_of(core * TOK, TOK), TOK)
    other = pl.ds(pl.multiple_of((1 - core) * TOK, TOK), TOK)
    for source, whose in ((ours, core), (theirs, 1 - core)):
        lanes = pl.ds(pl.multiple_of(whose * HALF, HALF), HALF)
        full[0:TOK, lanes] = source[mine, :]
        full[TOK:, lanes] = source[other, :]
    total = 0.0
    for weight, dy in zip(weights, (0, -1, 1, 2)):
        deep = weight.shape[0]
        start = lax.rem(row + dy + rows_of, rows_of) * deep
        left = full[:, pl.ds(pl.multiple_of(start, 128), deep)]
        total = total + jnp.dot(left, weight[...], preferred_element_type=F32)
    each = TOK // len(outs)
    for k, out in enumerate(outs):
        for low in range(2):
            out[low * each : (low + 1) * each] = total[low * TOK + k * each : low * TOK + (k + 1) * each].astype(BF16)


def whole_block(shape):
    return pl.BlockSpec(shape, lambda i, info: (0,) * len(shape))


def core_block(shape):
    return pl.BlockSpec(shape, lambda i, info: (0,) * (len(shape) - 1) + (info[0],))


def call(kernel, name, info, args, in_specs, out_shape, out_specs, scratch=(), grid=1, flops=0, moved=0, vmem=VMEM):
    return pl.pallas_call(
        kernel,
        grid_spec=pltpu.PrefetchScalarGridSpec(
            num_scalar_prefetch=1, grid=(grid,), in_specs=in_specs, out_specs=out_specs, scratch_shapes=scratch
        ),
        out_shape=out_shape,
        compiler_params=pltpu.CompilerParams(vmem_limit_bytes=vmem),
        cost_estimate=pl.CostEstimate(flops=flops, bytes_accessed=moved, transcendentals=0),
        name=name,
    )(info, *args)


def tie(first, *rest):
    return lax.optimization_barrier((first, *rest))


def body(tokens, table, short_kernel, poles, residues, skip, out_weight):
    n_seq, n_tp = lax.axis_size("seq"), lax.axis_size("tp")
    chips = n_seq // 2
    ny = chips // NZ
    vocab, width = table.shape[0], out_weight.shape[1]
    index = lax.axis_index("seq")
    core, chip = index % 2, index // 2
    info = jnp.stack([core, chip, lax.axis_index("tp"), chip // NZ, chip % NZ]).astype(jnp.int32)
    swap = [(i, i ^ 1) for i in range(n_seq)]

    def move_y(value, d):
        return lax.ppermute(value, "seq", [(i, (i + d * 2 * NZ) % n_seq) for i in range(n_seq)])

    def move_z(value, d):
        pairs = [(i, i // (2 * NZ) * 2 * NZ + (i + 2 * d) % (2 * NZ)) for i in range(n_seq)]
        return lax.ppermute(value, "seq", pairs)

    def shifted(value, d):
        return lax.ppermute(value, "seq", [(i, i + 2 * d) for i in range(n_seq - 2 * d)])

    ids = tokens.reshape(1, TOK)
    before = lax.ppermute(ids, "seq", [(2 * p + 1, 2 * p + 2) for p in range(chips - 1)])
    cols = width // 2
    mine = lax.dynamic_slice_in_dim(out_weight, core * cols, cols, axis=1)
    came = lax.ppermute(lax.dynamic_slice_in_dim(out_weight, (1 - core) * cols, cols, axis=1), "seq", swap)
    block = jnp.concatenate([jnp.where(core == 0, mine, came), jnp.where(core == 0, came, mine)], axis=0)
    block, before = tie(block, before)
    other = lax.ppermute(jnp.concatenate([ids, before], axis=0), "seq", swap)
    ring = [block, move_z(block, 1), move_z(block, -1)]

    ids_block = whole_block((1, TOK))
    tok_block = whole_block((2 * TOK, HALF))
    flat_block = whole_block((4 * MODES, 128))
    flat = jax.ShapeDtypeStruct((4 * MODES, 128), F32)
    query, base, states, first = call(
        scan_kernel, "scan", info,
        (ids, other, before, jnp.transpose(table, (1, 0, 2)), short_kernel, poles, residues, skip.reshape(1, -1)),
        [ids_block, whole_block((2, TOK)), ids_block]
        + [core_block((3, vocab, HALF)), core_block((3, 3, HALF)), core_block((MODES, HALF)), core_block((MODES, HALF)), core_block((1, HALF))],
        (jax.ShapeDtypeStruct((2 * TOK, HALF), F32), jax.ShapeDtypeStruct((2 * TOK, HALF), F32), jax.ShapeDtypeStruct((chips, 4 * MODES, 128), BF16), flat),
        (tok_block, tok_block, whole_block((chips, 4 * MODES, 128)), flat_block),
        scratch=(
            pltpu.VMEM((3, 2 * TOK + 16, HALF), F32),
            pltpu.VMEM((8 * STEP, 128), F32),
            pltpu.VMEM((8 * STEP, 128), F32),
            pltpu.VMEM((MODES * 8, 128), F32),
            pltpu.VMEM((MODES * 8, 128), F32),
            pltpu.VMEM((MODES * 8, 128), F32),
        ),
        flops=600_000_000, moved=8_000_000,
    )
    states, *ring = tie(states, *ring)
    for _ in range(2):
        ring += [move_z(ring[-2], 1), move_z(ring[-1], -1)]
    part = cols // 2
    ring += [move_z(ring[-2][:, :part], 1), move_z(ring[-1][:, part:], -1)]
    part_rows = whole_block((32 * NZ, part))
    one, two = call(
        place_kernel, "place", info, ring,
        [whole_block((32, cols))] * 7 + [whole_block((32, part))] * 2,
        (jax.ShapeDtypeStruct((32 * NZ, part), BF16),) * 2,
        (part_rows,) * 2,
        flops=1_000_000, moved=2_000_000, vmem=VMEM // 3,
    )
    states, one, two = tie(states, one, two)
    up, down, down_two = move_y(one, 1), move_y(one, -1), move_y(two, -1)
    states = lax.all_to_all(
        states, "seq", 0, 0, axis_index_groups=[[2 * p + c for p in range(chips)] for c in range(2)]
    )
    two_late, up = tie(two, up)
    across_one = move_y(up, 1)
    up_two = move_y(two_late, 1)
    across_two = move_y(down_two, -1)
    weights = ((one, up, down, across_one), (two, up_two, down_two, across_two))
    gated = call(
        functools.partial(gate_kernel, n_tp), "gate", info, (states, first, poles, residues, query, base),
        [whole_block((chips, 4 * MODES, 128)), flat_block, core_block((MODES, HALF)), core_block((MODES, HALF)), tok_block, tok_block],
        jax.ShapeDtypeStruct((2 * TOK, HALF), BF16),
        tok_block,
        scratch=(
            pltpu.VMEM((MODES * 8, 128), F32),
            pltpu.VMEM((MODES * 8, 128), F32),
            pltpu.VMEM((8 * STEP, 128), F32),
            pltpu.VMEM((2 * TOK, HALF), F32),
        ),
        flops=20_000_000, moved=4_000_000,
    )
    partner = lax.ppermute(gated, "seq", swap)
    rows = TOK // n_tp
    tile = part // 2
    sides = ([], [])
    for group in weights:
        parts = call(
            functools.partial(project_kernel, ny), "project", info, (gated, partner, *group),
            [tok_block, tok_block] + [pl.BlockSpec((w.shape[0], tile), lambda i, info: (0, i)) for w in group],
            (jax.ShapeDtypeStruct((2 * rows, part), BF16),) * n_tp,
            (pl.BlockSpec((2 * rows, tile), lambda i, info: (0, i)),) * n_tp,
            scratch=(pltpu.VMEM((2 * TOK, 2 * HALF), BF16),),
            grid=part // tile, flops=4 * TOK * 2 * HALF * part, moved=2 * HALF * part * 2, vmem=VMEM // 3,
        )
        total = parts[0].astype(F32)
        for d in range(1, n_tp):
            total = total + lax.ppermute(parts[d], "tp", [(x, (x + d) % n_tp) for x in range(n_tp)]).astype(F32)
        total = total.astype(BF16)
        sides[0].append(total[:rows])
        sides[1].append(lax.ppermute(total[rows:], "seq", swap))
    return jnp.where(core == 0, jnp.concatenate(sides[0] + sides[1], axis=1), jnp.concatenate(sides[1] + sides[0], axis=1))


def solution(mesh):
    placed = (
        P("seq"),
        P(None, None, "tp"),
        P(None, None, "tp"),
        P(None, "tp"),
        P(None, "tp"),
        P("tp"),
        P(("tp", "seq"), None),
    )
    return jax.shard_map(
        body, mesh=mesh, in_specs=placed, out_specs=P(("seq", "tp"), None), check_vma=False
    )
```

time: 131 us -> 107 us (0.82)
  starting transfers between devices: 13.5 us -> 61 us
  waiting for transfers between devices: 55.5 us -> 24.3 us
  blocking collectives: 29.2 us -> 0 us
  between operations: 13.5 us -> 0.21 us
  Pallas kernels: 11.8 us -> 15.4 us
  local copies, waits for them, and re-layouts: 5.71 us -> 3 us
  other arithmetic: 0.91 us -> 2.46 us
    all_gather x1 -> x0, waiting for transfers between devices: 42 us -> none  [body(): weight = lax.all_gather(out_weight, 'seq', axis=0, tiled=True)]
    ppermute x3 -> x19, starting transfers between devices: 6.96 us -> 41.4 us  [the longest x8 12 us: move_z(): return lax.ppermute(value, 'seq', pairs)]
    all_to_all x1 -> x0, blocking collectives: 29.2 us -> none  [body(): lax.all_to_all(states, 'seq', 0, 0, axis_index_groups=[[2 * p + c for p i...]
    ppermute x3 -> x19, waiting for transfers between devices: 2.07 us -> 24.3 us  [the longest x6 14 us: move_y(): lax.ppermute(value, 'seq', [(i, (i + d * 2 * NZ) % n_seq) for i in range(...]
    ppermute x3 -> x6, waiting for transfers between devices: 10.6 us -> 0.02 us  [body(): lax.ppermute(parts[d], 'tp', [(x, (x + d) % n_tp) for x in range(n_tp)])]
    all_to_all x0 -> x1, starting transfers between devices: none -> 8.12 us  [body(): lax.all_to_all(states, 'seq', 0, 0, axis_index_groups=[[2 * p + c for p i...]
    ppermute x3 -> x6, starting transfers between devices: 4.85 us -> 9.79 us  [body(): lax.ppermute(parts[d], 'tp', [(x, (x + d) % n_tp) for x in range(n_tp)])]
    unnamed x12 -> x10, local copies, waits for them, and re-layouts: 5.71 us -> 1.52 us
  transfers between devices with their start and end apart: 8 -> 27, of which waited for: 5 -> 8; matrix products, arithmetic and copies ran while one was open for 0% -> 2% of each run, Pallas kernels for 3% -> 14%
where the time goes in v2:
time: 107 us; the launch traced here: 106 us
  starting transfers between devices  61 us (57%)
  waiting for transfers between devices  24.3 us (23%)
  Pallas kernels  15.4 us (14%)
  local copies, waits for them, and re-layouts  3 us (3%)
  other arithmetic  2.46 us (2%)
    pallas_call x5, Pallas kernels, call(): pl.pallas_call(kernel, grid_spec=pltpu.PrefetchScalarGridSpec(num_scalar_...  15.4 us
    ppermute x6, waiting for transfers between devices, move_y(): lax.ppermute(value, 'seq', [(i, (i + d * 2 * NZ) % n_seq) for i in range(...  14 us
    ppermute x8, starting transfers between devices, move_z(): return lax.ppermute(value, 'seq', pairs)  12 us
    ppermute x2, starting transfers between devices, body(): sides[1].append(lax.ppermute(total[rows:], 'seq', swap))  10.3 us
    ppermute x6, starting transfers between devices, body(): lax.ppermute(parts[d], 'tp', [(x, (x + d) % n_tp) for x in range(n_tp)])  9.79 us
    all_to_all x1, starting transfers between devices, body(): lax.all_to_all(states, 'seq', 0, 0, axis_index_groups=[[2 * p + c for p i...  8.12 us
    ppermute x8, waiting for transfers between devices, move_z(): return lax.ppermute(value, 'seq', pairs)  7.83 us
    ppermute x6, starting transfers between devices, move_y(): lax.ppermute(value, 'seq', [(i, (i + d * 2 * NZ) % n_seq) for i in range(...  6.67 us
  transfers between devices with their start and end apart: 27, of which 8 were waited for; matrix products, arithmetic and copies ran while one was open for 2% of the time, Pallas kernels for 14%

profile of v2, /device:TPU:1, one launch (start us, length us, event | category | flops | bytes accessed | tf_op | source)
XLA Modules:
  0.0 106.4 jit_solution(15049413339547610661)
XLA Ops:
  0.0 0.8 constant_dynamic-slice_fusion
  0.8 3.2 %collective-permute-start = (bf16[16,2048]{1,0:T(8,128)(2,1)S(1)}, bf16[16,2048]{1,0:T(8,128)(2,1)S(1)}, u32[]{:S(2)}, u32[]{:S(2)}) collective-permute-start(bf16[16,2048]{1,0:T(8,128)(2,1)S(1)} %constant_dynamic-slice_fusion), channel_id=1, source_target_pairs={{0,4},{4,0},{8,12},{12,8},{16,20},{20,16},{24,28},{28,24},{32,36},... | collective-permute-start | bytes 196616 | tf_op jit(solution)/shard_map/ppermute | solution.py:232
  4.1 1.7 %collective-permute-start.1 = (s32[1,128]{1,0:T(1,128)}, s32[1,128]{1,0:T(1,128)S(1)}, u32[]{:S(2)}, u32[]{:S(2)}) collective-permute-start(s32[1,128]{1,0:T(1,128)} %bitcast.10), channel_id=1, source_target_pairs={{4,8},{12,16},{20,24},{28,32},{36,40},{44,48},{52,56},{60,64},{68,... | collective-permute-start | bytes 1544 | tf_op jit(solution)/shard_map/ppermute | solution.py:229
  5.8 0.0 collective-permute-done
  5.8 0.9 broadcast_select_fusion.1
  6.7 0.0 collective-permute-done.1.passed
  6.7 3.5 %collective-permute-start.4 = (bf16[32,2048]{1,0:T(8,128)(2,1)S(1)}, bf16[32,2048]{1,0:T(8,128)(2,1)S(1)}, u32[]{:S(2)}, u32[]{:S(2)}) collective-permute-start(bf16[32,2048]{1,0:T(8,128)(2,1)S(1)} %pad_maximum_fusion.refs_0_), channel_id=1, source_target_pairs={{0,56},{4,60},{8,0},{12,4},{16,8},{20,12},{24,16},{28,20},{32,24},... | collective-permute-start | bytes 393224 | tf_op jit(solution)/shard_map/ppermute | solution.py:223
  10.3 0.0 collective-permute-start.3
  10.3 0.7 pad_add_fusion
  10.9 2.9 %collective-permute-start.2 = (s32[2,128]{1,0:T(2,128)S(1)}, s32[2,128]{1,0:T(2,128)S(1)}, u32[]{:S(2)}, u32[]{:S(2)}) collective-permute-start(s32[2,128]{1,0:T(2,128)S(1)} %pad_add_fusion), channel_id=1, source_target_pairs={{0,4},{4,0},{8,12},{12,8},{16,20},{20,16},{24,28},{28,24},{32,36},... | collective-permute-start | bytes 3080 | tf_op jit(solution)/shard_map/ppermute | solution.py:235
  13.9 0.6 stack.23.info
  14.5 0.2 collective-permute-done.2.other
  14.7 0.6 copy-done.4
  15.2 5.9 %scan.1 = (f32[256,512]{1,0:T(8,128)}, f32[256,512]{1,0:T(8,128)}, bf16[32,64,128]{2,1,0:T(8,128)(2,1)}, f32[64,128]{1,0:T(8,128)}) custom-call(s32[5]{0:T(128)} %stack.23.info, s32[1,128]{1,0:T(1,128)} %bitcast.12, s32[2,128]{1,0:T(2,128)} %copy-done.4, s32[1,128]{1,0:T(1,128)} %copy-done.3, bf16[3,512,1024]{2,1,0:T(8,128)(2,1)} %bitcast.8, ...), custom_call_target="tpu_custom_call" | custom-call | flops 600000000 | bytes 8000000 | tf_op jit(solution)/shard_map/scan/pallas_call | solution.py:192
  21.2 0.0 collective-permute-done.4.refs_2_
  21.2 0.0 collective-permute-done.3.refs_1_
  21.2 0.1 collective-permute-start.5
  21.3 3.0 %collective-permute-start.6 = (bf16[32,2048]{1,0:T(8,128)(2,1)S(1)}, bf16[32,2048]{1,0:T(8,128)(2,1)S(1)}, u32[]{:S(2)}, u32[]{:S(2)}) collective-permute-start(bf16[32,2048]{1,0:T(8,128)(2,1)S(1)} %collective-permute-done.4.refs_2_), channel_id=1, source_target_pairs={{0,56},{4,60},{8,0},{12,4},{16,8},{20,12},{24,16},{28,20},{32,24},... | collective-permute-start | bytes 393224 | tf_op jit(solution)/shard_map/ppermute | solution.py:223
  24.3 3.5 %collective-permute-done.5.refs_3_ = bf16[32,2048]{1,0:T(8,128)(2,1)S(1)} collective-permute-done((bf16[32,2048]{1,0:T(8,128)(2,1)S(1)}, bf16[32,2048]{1,0:T(8,128)(2,1)S(1)}, u32[]{:S(2)}, u32[]{:S(2)}) %collective-permute-start.5) | collective-permute-done | bytes 131104 | tf_op jit(solution)/shard_map/ppermute | solution.py:223
  27.8 0.0 collective-permute-start.7
  27.8 0.0 collective-permute-done.6.refs_4_
  27.8 2.7 %collective-permute-start.8 = (bf16[32,2048]{1,0:T(8,128)(2,1)S(1)}, bf16[32,2048]{1,0:T(8,128)(2,1)S(1)}, u32[]{:S(2)}, u32[]{:S(2)}) collective-permute-start(bf16[32,2048]{1,0:T(8,128)(2,1)S(1)} %collective-permute-done.6.refs_4_), channel_id=1, source_target_pairs={{0,56},{4,60},{8,0},{12,4},{16,8},{20,12},{24,16},{28,20},{32,24},... | collective-permute-start | bytes 393224 | tf_op jit(solution)/shard_map/ppermute | solution.py:223
  30.5 2.7 %collective-permute-done.7.refs_5_ = bf16[32,2048]{1,0:T(8,128)(2,1)S(1)} collective-permute-done((bf16[32,2048]{1,0:T(8,128)(2,1)S(1)}, bf16[32,2048]{1,0:T(8,128)(2,1)S(1)}, u32[]{:S(2)}, u32[]{:S(2)}) %collective-permute-start.7) | collective-permute-done | bytes 131104 | tf_op jit(solution)/shard_map/ppermute | solution.py:223
  33.3 2.7 %collective-permute-start.10 = (bf16[32,1024]{1,0:T(8,128)(2,1)S(1)}, bf16[32,1024]{1,0:T(8,128)(2,1)S(1)}, u32[]{:S(2)}, u32[]{:S(2)}) collective-permute-start(bf16[32,1024]{1,0:T(8,128)(2,1)S(1)} %slice.25), channel_id=1, source_target_pairs={{0,56},{4,60},{8,0},{12,4},{16,8},{20,12},{24,16},{28,20},{32,24},... | collective-permute-start | bytes 196616 | tf_op jit(solution)/shard_map/ppermute | solution.py:223
  36.0 1.6 %collective-permute-done.9.refs_7_ = bf16[32,1024]{1,0:T(8,128)(2,1)S(1)} collective-permute-done((bf16[32,1024]{1,0:T(8,128)(2,1)S(1)}, bf16[32,1024]{1,0:T(8,128)(2,1)S(1)}, u32[]{:S(2)}, u32[]{:S(2)}) %collective-permute-start.9) | collective-permute-done | bytes 65568 | tf_op jit(solution)/shard_map/ppermute | solution.py:223
  37.6 0.0 collective-permute-done.10.refs_8_
  37.6 0.6 place.1
  38.2 8.1 %all-to-all-start = ((bf16[32,64,128]{2,1,0:T(8,128)(2,1)}), bf16[32,64,128]{2,1,0:T(8,128)(2,1)}, u32[]{:S(2)}, u32[]{:S(2)}) async-start(bf16[32,64,128]{2,1,0:T(8,128)(2,1)} %get-tuple-element.39), calls=%async_computation | async-start | bytes 1048576 | tf_op jit(solution)/shard_map/all_to_all | solution.py:274
  46.3 1.2 %collective-permute-start.12 = (bf16[256,1024]{1,0:T(8,128)(2,1)S(1)}, bf16[256,1024]{1,0:T(8,128)(2,1)}, u32[]{:S(2)}, u32[]{:S(2)}) collective-permute-start(bf16[256,1024]{1,0:T(8,128)(2,1)S(1)} %get-tuple-element.43.refs_0_), channel_id=1, source_target_pairs={{0,64},{4,68},{8,72},{12,76},{16,80},{20,84},{24,88},{28,92},{32,9... | collective-permute-start | bytes 1572872 | tf_op jit(solution)/shard_map/ppermute | solution.py:219
  47.6 1.5 %collective-permute-start.19 = (bf16[256,1024]{1,0:T(8,128)(2,1)S(1)}, bf16[256,1024]{1,0:T(8,128)(2,1)S(1)}, u32[]{:S(2)}, u32[]{:S(2)}) collective-permute-start(bf16[256,1024]{1,0:T(8,128)(2,1)S(1)} %get-tuple-element.50.refs_0_), channel_id=1, source_target_pairs={{0,192},{4,196},{8,200},{12,204},{16,208},{20,212},{24,216},{28,22... | collective-permute-start | bytes 1572872 | tf_op jit(solution)/shard_map/ppermute | solution.py:219
  49.1 1.2 %collective-permute-start.13 = (bf16[256,1024]{1,0:T(8,128)(2,1)S(1)}, bf16[256,1024]{1,0:T(8,128)(2,1)}, u32[]{:S(2)}, u32[]{:S(2)}) collective-permute-start(bf16[256,1024]{1,0:T(8,128)(2,1)S(1)} %get-tuple-element.43.refs_0_), channel_id=1, source_target_pairs={{0,192},{4,196},{8,200},{12,204},{16,208},{20,212},{24,216},{28,22... | collective-permute-start | bytes 1572872 | tf_op jit(solution)/shard_map/ppermute | solution.py:219
  50.3 13.7 %collective-permute-done.12.refs_1_ = bf16[256,1024]{1,0:T(8,128)(2,1)} collective-permute-done((bf16[256,1024]{1,0:T(8,128)(2,1)S(1)}, bf16[256,1024]{1,0:T(8,128)(2,1)}, u32[]{:S(2)}, u32[]{:S(2)}) %collective-permute-start.12) | collective-permute-done | bytes 524320 | tf_op jit(solution)/shard_map/ppermute | solution.py:219
  64.0 0.0 collective-permute-start.14
  64.0 1.1 %collective-permute-start.18 = (bf16[256,1024]{1,0:T(8,128)(2,1)S(1)}, bf16[256,1024]{1,0:T(8,128)(2,1)}, u32[]{:S(2)}, u32[]{:S(2)}) collective-permute-start(bf16[256,1024]{1,0:T(8,128)(2,1)S(1)} %get-tuple-element.50.refs_0_), channel_id=1, source_target_pairs={{0,64},{4,68},{8,72},{12,76},{16,80},{20,84},{24,88},{28,92},{32,9... | collective-permute-start | bytes 1572872 | tf_op jit(solution)/shard_map/ppermute | solution.py:219
  65.1 0.0 collective-permute-done.19.refs_2_
  65.1 1.6 %collective-permute-start.20 = (bf16[256,1024]{1,0:T(8,128)(2,1)S(1)}, bf16[256,1024]{1,0:T(8,128)(2,1)}, u32[]{:S(2)}, u32[]{:S(2)}) collective-permute-start(bf16[256,1024]{1,0:T(8,128)(2,1)S(1)} %collective-permute-done.19.refs_2_), channel_id=1, source_target_pairs={{0,192},{4,196},{8,200},{12,204},{16,208},{20,212},{24,216},{28,22... | collective-permute-start | bytes 1572872 | tf_op jit(solution)/shard_map/ppermute | solution.py:219
  66.7 0.0 all-to-all-done.states
  66.7 3.5 %gate.1.ours = bf16[256,512]{1,0:T(8,128)(2,1)} custom-call(s32[5]{0:T(128)} %stack.23.info, bf16[32,64,128]{2,1,0:T(8,128)(2,1)} %all-to-all-done.states, f32[64,128]{1,0:T(8,128)} %get-tuple-element.40.first, f32[16,1024]{1,0:T(8,128)} %poles.3, f32[16,1024]{1,0:T(8,128)} %residues.3, f32[256,512]{1,0:T(8,128)} %get-tuple-element.41.query, ...), custom_call_target="tpu_custom_call" | custom-call | flops 20000000 | bytes 4000000 | tf_op jit(solution)/shard_map/gate/pallas_call | solution.py:192
  70.3 6.2 %collective-permute-start.11 = (bf16[256,512]{1,0:T(8,128)(2,1)}, bf16[256,512]{1,0:T(8,128)(2,1)S(1)}, u32[]{:S(2)}, u32[]{:S(2)}) collective-permute-start(bf16[256,512]{1,0:T(8,128)(2,1)} %gate.1.ours), channel_id=1, source_target_pairs={{0,4},{4,0},{8,12},{12,8},{16,20},{20,16},{24,28},{28,24},{32,36},... | collective-permute-start | bytes 786440 | tf_op jit(solution)/shard_map/ppermute | solution.py:295
  76.4 0.0 collective-permute-done.13.refs_2_
  76.4 0.0 collective-permute-done.14.refs_3_
  76.4 1.4 %collective-permute-done.11.theirs = bf16[256,512]{1,0:T(8,128)(2,1)S(1)} collective-permute-done((bf16[256,512]{1,0:T(8,128)(2,1)}, bf16[256,512]{1,0:T(8,128)(2,1)S(1)}, u32[]{:S(2)}, u32[]{:S(2)}) %collective-permute-start.11) | collective-permute-done | bytes 262176 | tf_op jit(solution)/shard_map/ppermute | solution.py:295
  77.8 0.9 copy-done
  78.7 2.7 %project.2 = (bf16[64,1024]{1,0:T(8,128)(2,1)S(1)}, bf16[64,1024]{1,0:T(8,128)(2,1)S(1)}, bf16[64,1024]{1,0:T(8,128)(2,1)S(1)}, bf16[64,1024]{1,0:T(8,128)(2,1)S(1)}) custom-call(s32[5]{0:T(128)S(1)} %copy-done.2, bf16[256,512]{1,0:T(8,128)(2,1)S(1)} %copy-done, bf16[256,512]{1,0:T(8,128)(2,1)S(1)} %collective-permute-done.11.theirs, ...), custom_call_target="tpu_custom_call" | custom-call | flops 536870912 | bytes 2097152 | tf_op jit(solution)/shard_map/project/pallas_call | solution.py:192
  81.5 1.3 %collective-permute-start.15 = (bf16[64,1024]{1,0:T(8,128)(2,1)S(1)}, bf16[64,1024]{1,0:T(8,128)(2,1)S(1)}, u32[]{:S(2)}, u32[]{:S(2)}) collective-permute-start(bf16[64,1024]{1,0:T(8,128)(2,1)S(1)} %get-tuple-element.47), channel_id=1, source_target_pairs={{0,1},{1,2},{2,3},{3,0},{4,5},{5,6},{6,7},{7,4},{8,9},{9,10},{10,1... | collective-permute-start | bytes 393224 | tf_op jit(solution)/shard_map/ppermute | solution.py:310
  82.8 2.4 %collective-permute-start.16 = (bf16[64,1024]{1,0:T(8,128)(2,1)S(1)}, bf16[64,1024]{1,0:T(8,128)(2,1)S(1)}, u32[]{:S(2)}, u32[]{:S(2)}) collective-permute-start(bf16[64,1024]{1,0:T(8,128)(2,1)S(1)} %get-tuple-element.48), channel_id=1, source_target_pairs={{0,2},{1,3},{2,0},{3,1},{4,6},{5,7},{6,4},{7,5},{8,10},{9,11},{10,... | collective-permute-start | bytes 393224 | tf_op jit(solution)/shard_map/ppermute | solution.py:310
  85.2 1.2 %collective-permute-start.17 = (bf16[64,1024]{1,0:T(8,128)(2,1)S(1)}, bf16[64,1024]{1,0:T(8,128)(2,1)S(1)}, u32[]{:S(2)}, u32[]{:S(2)}) collective-permute-start(bf16[64,1024]{1,0:T(8,128)(2,1)S(1)} %get-tuple-element.49), channel_id=1, source_target_pairs={{0,3},{1,0},{2,1},{3,2},{4,7},{5,4},{6,5},{7,6},{8,11},{9,8},{10,9... | collective-permute-start | bytes 393224 | tf_op jit(solution)/shard_map/ppermute | solution.py:310
  86.4 0.3 collective-permute-done.18.refs_1_
  86.7 2.6 %project.3 = (bf16[64,1024]{1,0:T(8,128)(2,1)S(1)}, bf16[64,1024]{1,0:T(8,128)(2,1)S(1)}, bf16[64,1024]{1,0:T(8,128)(2,1)S(1)}, bf16[64,1024]{1,0:T(8,128)(2,1)S(1)}) custom-call(s32[5]{0:T(128)S(1)} %copy-done.2, bf16[256,512]{1,0:T(8,128)(2,1)S(1)} %copy-done, bf16[256,512]{1,0:T(8,128)(2,1)S(1)} %collective-permute-done.11.theirs, ...), custom_call_target="tpu_custom_call" | custom-call | flops 536870912 | bytes 2097152 | tf_op jit(solution)/shard_map/project/pallas_call | solution.py:192
  89.3 1.3 %collective-permute-start.21 = (bf16[64,1024]{1,0:T(8,128)(2,1)S(1)}, bf16[64,1024]{1,0:T(8,128)(2,1)S(1)}, u32[]{:S(2)}, u32[]{:S(2)}) collective-permute-start(bf16[64,1024]{1,0:T(8,128)(2,1)S(1)} %get-tuple-element.52), channel_id=1, source_target_pairs={{0,1},{1,2},{2,3},{3,0},{4,5},{5,6},{6,7},{7,4},{8,9},{9,10},{10,1... | collective-permute-start | bytes 393224 | tf_op jit(solution)/shard_map/ppermute | solution.py:310
  90.6 2.5 %collective-permute-start.22 = (bf16[64,1024]{1,0:T(8,128)(2,1)S(1)}, bf16[64,1024]{1,0:T(8,128)(2,1)S(1)}, u32[]{:S(2)}, u32[]{:S(2)}) collective-permute-start(bf16[64,1024]{1,0:T(8,128)(2,1)S(1)} %get-tuple-element.53), channel_id=1, source_target_pairs={{0,2},{1,3},{2,0},{3,1},{4,6},{5,7},{6,4},{7,5},{8,10},{9,11},{10,... | collective-permute-start | bytes 393224 | tf_op jit(solution)/shard_map/ppermute | solution.py:310
  93.0 1.1 %collective-permute-start.23 = (bf16[64,1024]{1,0:T(8,128)(2,1)S(1)}, bf16[64,1024]{1,0:T(8,128)(2,1)S(1)}, u32[]{:S(2)}, u32[]{:S(2)}) collective-permute-start(bf16[64,1024]{1,0:T(8,128)(2,1)S(1)} %get-tuple-element.54), channel_id=1, source_target_pairs={{0,3},{1,0},{2,1},{3,2},{4,7},{5,4},{6,5},{7,6},{8,11},{9,8},{10,9... | collective-permute-start | bytes 393224 | tf_op jit(solution)/shard_map/ppermute | solution.py:310
  94.2 0.0 collective-permute-done.16
  94.2 0.0 collective-permute-done.17
  94.2 0.1 add_convert_fusion.1
  94.3 5.4 %collective-permute-start.24 = (bf16[32,1024]{1,0:T(8,128)(2,1)S(1)}, bf16[32,1024]{1,0:T(8,128)(2,1)S(1)}, u32[]{:S(2)}, u32[]{:S(2)}) collective-permute-start(bf16[32,1024]{1,0:T(8,128)(2,1)S(1)} %get-tuple-element.58), channel_id=1, source_target_pairs={{0,4},{4,0},{8,12},{12,8},{16,20},{20,16},{24,28},{28,24},{32,36},... | collective-permute-start | bytes 196616 | tf_op jit(solution)/shard_map/ppermute | solution.py:313
  99.6 0.0 collective-permute-done.21
  99.6 0.0 collective-permute-done.22
  99.6 0.0 collective-permute-done.23
  99.7 0.1 add_convert_fusion
  99.8 4.9 %collective-permute-start.25 = (bf16[32,1024]{1,0:T(8,128)(2,1)S(1)}, bf16[32,1024]{1,0:T(8,128)(2,1)S(1)}, u32[]{:S(2)}, u32[]{:S(2)}) collective-permute-start(bf16[32,1024]{1,0:T(8,128)(2,1)S(1)} %get-tuple-element.60), channel_id=1, source_target_pairs={{0,4},{4,0},{8,12},{12,8},{16,20},{20,16},{24,28},{28,24},{32,36},... | collective-permute-start | bytes 196616 | tf_op jit(solution)/shard_map/ppermute | solution.py:313
  104.7 0.0 collective-permute-done.24
  104.7 0.9 collective-permute-done.25
  105.6 0.8 maximum_select_fusion
  (17 shorter events, 0.1 us)
Async XLA Ops:
  0.8 5.0 %collective-permute-start = (bf16[16,2048]{1,0:T(8,128)(2,1)S(1)}, bf16[16,2048]{1,0:T(8,128)(2,1)S(1)}, u32[]{:S(2)}, u32[]{:S(2)}) collective-permute-start(bf16[16,2048]{1,0:T(8,128)(2,1)S(1)} %constant_dynamic-slice_fusion), channel_id=1, source_target_pairs={{0,4},{4,0},{8,12},{12,8},{16,20},{20,16},{24,28},{28,24},{32,36},... | collective-permute-start | bytes 196616 | tf_op jit(solution)/shard_map/ppermute | solution.py:232
  4.1 2.6 %collective-permute-start.1 = (s32[1,128]{1,0:T(1,128)}, s32[1,128]{1,0:T(1,128)S(1)}, u32[]{:S(2)}, u32[]{:S(2)}) collective-permute-start(s32[1,128]{1,0:T(1,128)} %bitcast.10), channel_id=1, source_target_pairs={{4,8},{12,16},{20,24},{28,32},{36,40},{44,48},{52,56},{60,64},{68,... | collective-permute-start | bytes 1544 | tf_op jit(solution)/shard_map/ppermute | solution.py:229
  6.7 8.0 %copy-start.3 = (s32[1,128]{1,0:T(1,128)}, s32[1,128]{1,0:T(1,128)S(1)}, u32[]{:S(2)}) copy-start(s32[1,128]{1,0:T(1,128)S(1)} %collective-permute-done.1.passed) | copy-start | bytes 1540
  6.7 14.4 %collective-permute-start.4 = (bf16[32,2048]{1,0:T(8,128)(2,1)S(1)}, bf16[32,2048]{1,0:T(8,128)(2,1)S(1)}, u32[]{:S(2)}, u32[]{:S(2)}) collective-permute-start(bf16[32,2048]{1,0:T(8,128)(2,1)S(1)} %pad_maximum_fusion.refs_0_), channel_id=1, source_target_pairs={{0,56},{4,60},{8,0},{12,4},{16,8},{20,12},{24,16},{28,20},{32,24},... | collective-permute-start | bytes 393224 | tf_op jit(solution)/shard_map/ppermute | solution.py:223
  10.3 10.9 %collective-permute-start.3 = (bf16[32,2048]{1,0:T(8,128)(2,1)S(1)}, bf16[32,2048]{1,0:T(8,128)(2,1)S(1)}, u32[]{:S(2)}, u32[]{:S(2)}) collective-permute-start(bf16[32,2048]{1,0:T(8,128)(2,1)S(1)} %pad_maximum_fusion.refs_0_), channel_id=1, source_target_pairs={{0,8},{4,12},{8,16},{12,20},{16,24},{20,28},{24,32},{28,36},{32,40... | collective-permute-start | bytes 393224 | tf_op jit(solution)/shard_map/ppermute | solution.py:223
  10.9 3.8 %collective-permute-start.2 = (s32[2,128]{1,0:T(2,128)S(1)}, s32[2,128]{1,0:T(2,128)S(1)}, u32[]{:S(2)}, u32[]{:S(2)}) collective-permute-start(s32[2,128]{1,0:T(2,128)S(1)} %pad_add_fusion), channel_id=1, source_target_pairs={{0,4},{4,0},{8,12},{12,8},{16,20},{20,16},{24,28},{28,24},{32,36},... | collective-permute-start | bytes 3080 | tf_op jit(solution)/shard_map/ppermute | solution.py:235
  14.5 23.1 %copy-start.1 = (s32[5]{0:T(128)S(1)}, s32[5]{0:T(128)}, u32[]{:S(2)}) copy-start(s32[5]{0:T(128)} %stack.23.info) | copy-start | bytes 64
  14.7 0.6 copy-start.4
  15.2 62.5 %copy-start.2 = (s32[5]{0:T(128)S(1)}, s32[5]{0:T(128)}, u32[]{:S(2)}) copy-start(s32[5]{0:T(128)} %stack.23.info) | copy-start | bytes 64
  21.2 6.7 %collective-permute-start.5 = (bf16[32,2048]{1,0:T(8,128)(2,1)S(1)}, bf16[32,2048]{1,0:T(8,128)(2,1)S(1)}, u32[]{:S(2)}, u32[]{:S(2)}) collective-permute-start(bf16[32,2048]{1,0:T(8,128)(2,1)S(1)} %collective-permute-done.3.refs_1_), channel_id=1, source_target_pairs={{0,8},{4,12},{8,16},{12,20},{16,24},{20,28},{24,32},{28,36},{32,40... | collective-permute-start | bytes 393224 | tf_op jit(solution)/shard_map/ppermute | solution.py:223
  21.3 6.6 %collective-permute-start.6 = (bf16[32,2048]{1,0:T(8,128)(2,1)S(1)}, bf16[32,2048]{1,0:T(8,128)(2,1)S(1)}, u32[]{:S(2)}, u32[]{:S(2)}) collective-permute-start(bf16[32,2048]{1,0:T(8,128)(2,1)S(1)} %collective-permute-done.4.refs_2_), channel_id=1, source_target_pairs={{0,56},{4,60},{8,0},{12,4},{16,8},{20,12},{24,16},{28,20},{32,24},... | collective-permute-start | bytes 393224 | tf_op jit(solution)/shard_map/ppermute | solution.py:223
  27.8 5.4 %collective-permute-start.7 = (bf16[32,2048]{1,0:T(8,128)(2,1)S(1)}, bf16[32,2048]{1,0:T(8,128)(2,1)S(1)}, u32[]{:S(2)}, u32[]{:S(2)}) collective-permute-start(bf16[32,2048]{1,0:T(8,128)(2,1)S(1)} %collective-permute-done.5.refs_3_), channel_id=1, source_target_pairs={{0,8},{4,12},{8,16},{12,20},{16,24},{20,28},{24,32},{28,36},{32,40... | collective-permute-start | bytes 393224 | tf_op jit(solution)/shard_map/ppermute | solution.py:223
  27.8 5.4 %collective-permute-start.8 = (bf16[32,2048]{1,0:T(8,128)(2,1)S(1)}, bf16[32,2048]{1,0:T(8,128)(2,1)S(1)}, u32[]{:S(2)}, u32[]{:S(2)}) collective-permute-start(bf16[32,2048]{1,0:T(8,128)(2,1)S(1)} %collective-permute-done.6.refs_4_), channel_id=1, source_target_pairs={{0,56},{4,60},{8,0},{12,4},{16,8},{20,12},{24,16},{28,20},{32,24},... | collective-permute-start | bytes 393224 | tf_op jit(solution)/shard_map/ppermute | solution.py:223
  33.2 4.3 %collective-permute-start.9 = (bf16[32,1024]{1,0:T(8,128)(2,1)S(1)}, bf16[32,1024]{1,0:T(8,128)(2,1)S(1)}, u32[]{:S(2)}, u32[]{:S(2)}) collective-permute-start(bf16[32,1024]{1,0:T(8,128)(2,1)S(1)} %slice.24), channel_id=1, source_target_pairs={{0,8},{4,12},{8,16},{12,20},{16,24},{20,28},{24,32},{28,36},{32,40... | collective-permute-start | bytes 196616 | tf_op jit(solution)/shard_map/ppermute | solution.py:223
  33.3 4.3 %collective-permute-start.10 = (bf16[32,1024]{1,0:T(8,128)(2,1)S(1)}, bf16[32,1024]{1,0:T(8,128)(2,1)S(1)}, u32[]{:S(2)}, u32[]{:S(2)}) collective-permute-start(bf16[32,1024]{1,0:T(8,128)(2,1)S(1)} %slice.25), channel_id=1, source_target_pairs={{0,56},{4,60},{8,0},{12,4},{16,8},{20,12},{24,16},{28,20},{32,24},... | collective-permute-start | bytes 196616 | tf_op jit(solution)/shard_map/ppermute | solution.py:223
  38.2 28.5 %all-to-all-start = ((bf16[32,64,128]{2,1,0:T(8,128)(2,1)}), bf16[32,64,128]{2,1,0:T(8,128)(2,1)}, u32[]{:S(2)}, u32[]{:S(2)}) async-start(bf16[32,64,128]{2,1,0:T(8,128)(2,1)} %get-tuple-element.39), calls=%async_computation | async-start | bytes 1048576 | tf_op jit(solution)/shard_map/all_to_all | solution.py:274
  46.3 17.7 %collective-permute-start.12 = (bf16[256,1024]{1,0:T(8,128)(2,1)S(1)}, bf16[256,1024]{1,0:T(8,128)(2,1)}, u32[]{:S(2)}, u32[]{:S(2)}) collective-permute-start(bf16[256,1024]{1,0:T(8,128)(2,1)S(1)} %get-tuple-element.43.refs_0_), channel_id=1, source_target_pairs={{0,64},{4,68},{8,72},{12,76},{16,80},{20,84},{24,88},{28,92},{32,9... | collective-permute-start | bytes 1572872 | tf_op jit(solution)/shard_map/ppermute | solution.py:219
  47.6 17.6 %collective-permute-start.19 = (bf16[256,1024]{1,0:T(8,128)(2,1)S(1)}, bf16[256,1024]{1,0:T(8,128)(2,1)S(1)}, u32[]{:S(2)}, u32[]{:S(2)}) collective-permute-start(bf16[256,1024]{1,0:T(8,128)(2,1)S(1)} %get-tuple-element.50.refs_0_), channel_id=1, source_target_pairs={{0,192},{4,196},{8,200},{12,204},{16,208},{20,212},{24,216},{28,22... | collective-permute-start | bytes 1572872 | tf_op jit(solution)/shard_map/ppermute | solution.py:219
  49.1 27.3 %collective-permute-start.13 = (bf16[256,1024]{1,0:T(8,128)(2,1)S(1)}, bf16[256,1024]{1,0:T(8,128)(2,1)}, u32[]{:S(2)}, u32[]{:S(2)}) collective-permute-start(bf16[256,1024]{1,0:T(8,128)(2,1)S(1)} %get-tuple-element.43.refs_0_), channel_id=1, source_target_pairs={{0,192},{4,196},{8,200},{12,204},{16,208},{20,212},{24,216},{28,22... | collective-permute-start | bytes 1572872 | tf_op jit(solution)/shard_map/ppermute | solution.py:219
  64.0 12.4 %collective-permute-start.14 = (bf16[256,1024]{1,0:T(8,128)(2,1)}, bf16[256,1024]{1,0:T(8,128)(2,1)}, u32[]{:S(2)}, u32[]{:S(2)}) collective-permute-start(bf16[256,1024]{1,0:T(8,128)(2,1)} %collective-permute-done.12.refs_1_), channel_id=1, source_target_pairs={{0,64},{4,68},{8,72},{12,76},{16,80},{20,84},{24,88},{28,92},{32,9... | collective-permute-start | bytes 1572872 | tf_op jit(solution)/shard_map/ppermute | solution.py:219
  64.0 22.7 %collective-permute-start.18 = (bf16[256,1024]{1,0:T(8,128)(2,1)S(1)}, bf16[256,1024]{1,0:T(8,128)(2,1)}, u32[]{:S(2)}, u32[]{:S(2)}) collective-permute-start(bf16[256,1024]{1,0:T(8,128)(2,1)S(1)} %get-tuple-element.50.refs_0_), channel_id=1, source_target_pairs={{0,64},{4,68},{8,72},{12,76},{16,80},{20,84},{24,88},{28,92},{32,9... | collective-permute-start | bytes 1572872 | tf_op jit(solution)/shard_map/ppermute | solution.py:219
  65.1 21.5 %collective-permute-start.20 = (bf16[256,1024]{1,0:T(8,128)(2,1)S(1)}, bf16[256,1024]{1,0:T(8,128)(2,1)}, u32[]{:S(2)}, u32[]{:S(2)}) collective-permute-start(bf16[256,1024]{1,0:T(8,128)(2,1)S(1)} %collective-permute-done.19.refs_2_), channel_id=1, source_target_pairs={{0,192},{4,196},{8,200},{12,204},{16,208},{20,212},{24,216},{28,22... | collective-permute-start | bytes 1572872 | tf_op jit(solution)/shard_map/ppermute | solution.py:219
  70.3 7.5 %collective-permute-start.11 = (bf16[256,512]{1,0:T(8,128)(2,1)}, bf16[256,512]{1,0:T(8,128)(2,1)S(1)}, u32[]{:S(2)}, u32[]{:S(2)}) collective-permute-start(bf16[256,512]{1,0:T(8,128)(2,1)} %gate.1.ours), channel_id=1, source_target_pairs={{0,4},{4,0},{8,12},{12,8},{16,20},{20,16},{24,28},{28,24},{32,36},... | collective-permute-start | bytes 786440 | tf_op jit(solution)/shard_map/ppermute | solution.py:295
  77.8 1.0 copy-start
  81.5 11.6 %collective-permute-start.15 = (bf16[64,1024]{1,0:T(8,128)(2,1)S(1)}, bf16[64,1024]{1,0:T(8,128)(2,1)S(1)}, u32[]{:S(2)}, u32[]{:S(2)}) collective-permute-start(bf16[64,1024]{1,0:T(8,128)(2,1)S(1)} %get-tuple-element.47), channel_id=1, source_target_pairs={{0,1},{1,2},{2,3},{3,0},{4,5},{5,6},{6,7},{7,4},{8,9},{9,10},{10,1... | collective-permute-start | bytes 393224 | tf_op jit(solution)/shard_map/ppermute | solution.py:310
  82.8 11.4 %collective-permute-start.16 = (bf16[64,1024]{1,0:T(8,128)(2,1)S(1)}, bf16[64,1024]{1,0:T(8,128)(2,1)S(1)}, u32[]{:S(2)}, u32[]{:S(2)}) collective-permute-start(bf16[64,1024]{1,0:T(8,128)(2,1)S(1)} %get-tuple-element.48), channel_id=1, source_target_pairs={{0,2},{1,3},{2,0},{3,1},{4,6},{5,7},{6,4},{7,5},{8,10},{9,11},{10,... | collective-permute-start | bytes 393224 | tf_op jit(solution)/shard_map/ppermute | solution.py:310
  85.2 9.0 %collective-permute-start.17 = (bf16[64,1024]{1,0:T(8,128)(2,1)S(1)}, bf16[64,1024]{1,0:T(8,128)(2,1)S(1)}, u32[]{:S(2)}, u32[]{:S(2)}) collective-permute-start(bf16[64,1024]{1,0:T(8,128)(2,1)S(1)} %get-tuple-element.49), channel_id=1, source_target_pairs={{0,3},{1,0},{2,1},{3,2},{4,7},{5,4},{6,5},{7,6},{8,11},{9,8},{10,9... | collective-permute-start | bytes 393224 | tf_op jit(solution)/shard_map/ppermute | solution.py:310
  89.3 10.4 %collective-permute-start.21 = (bf16[64,1024]{1,0:T(8,128)(2,1)S(1)}, bf16[64,1024]{1,0:T(8,128)(2,1)S(1)}, u32[]{:S(2)}, u32[]{:S(2)}) collective-permute-start(bf16[64,1024]{1,0:T(8,128)(2,1)S(1)} %get-tuple-element.52), channel_id=1, source_target_pairs={{0,1},{1,2},{2,3},{3,0},{4,5},{5,6},{6,7},{7,4},{8,9},{9,10},{10,1... | collective-permute-start | bytes 393224 | tf_op jit(solution)/shard_map/ppermute | solution.py:310
  90.6 9.1 %collective-permute-start.22 = (bf16[64,1024]{1,0:T(8,128)(2,1)S(1)}, bf16[64,1024]{1,0:T(8,128)(2,1)S(1)}, u32[]{:S(2)}, u32[]{:S(2)}) collective-permute-start(bf16[64,1024]{1,0:T(8,128)(2,1)S(1)} %get-tuple-element.53), channel_id=1, source_target_pairs={{0,2},{1,3},{2,0},{3,1},{4,6},{5,7},{6,4},{7,5},{8,10},{9,11},{10,... | collective-permute-start | bytes 393224 | tf_op jit(solution)/shard_map/ppermute | solution.py:310
  93.0 6.6 %collective-permute-start.23 = (bf16[64,1024]{1,0:T(8,128)(2,1)S(1)}, bf16[64,1024]{1,0:T(8,128)(2,1)S(1)}, u32[]{:S(2)}, u32[]{:S(2)}) collective-permute-start(bf16[64,1024]{1,0:T(8,128)(2,1)S(1)} %get-tuple-element.54), channel_id=1, source_target_pairs={{0,3},{1,0},{2,1},{3,2},{4,7},{5,4},{6,5},{7,6},{8,11},{9,8},{10,9... | collective-permute-start | bytes 393224 | tf_op jit(solution)/shard_map/ppermute | solution.py:310
  94.3 10.4 %collective-permute-start.24 = (bf16[32,1024]{1,0:T(8,128)(2,1)S(1)}, bf16[32,1024]{1,0:T(8,128)(2,1)S(1)}, u32[]{:S(2)}, u32[]{:S(2)}) collective-permute-start(bf16[32,1024]{1,0:T(8,128)(2,1)S(1)} %get-tuple-element.58), channel_id=1, source_target_pairs={{0,4},{4,0},{8,12},{12,8},{16,20},{20,16},{24,28},{28,24},{32,36},... | collective-permute-start | bytes 196616 | tf_op jit(solution)/shard_map/ppermute | solution.py:313
  99.8 5.8 %collective-permute-start.25 = (bf16[32,1024]{1,0:T(8,128)(2,1)S(1)}, bf16[32,1024]{1,0:T(8,128)(2,1)S(1)}, u32[]{:S(2)}, u32[]{:S(2)}) collective-permute-start(bf16[32,1024]{1,0:T(8,128)(2,1)S(1)} %get-tuple-element.60), channel_id=1, source_target_pairs={{0,4},{4,0},{8,12},{12,8},{16,20},{20,16},{24,28},{28,24},{32,36},... | collective-permute-start | bytes 196616 | tf_op jit(solution)/shard_map/ppermute | solution.py:313

commit v3 on v2

--- a/solution.py
+++ b/solution.py
@@ -34,15 +34,15 @@
 
 
 def scan_kernel(
-    info, own, other, passed, table, taps, poles, residues, skip,
+    info, own, other, before_near, before_far, table, taps, poles, residues, skip,
     query_out, base_out, states_out, first_out,
     streams, drive_scr, filt_scr, pole_scr, res_scr, state_scr,
 ):
     core, chip = info[0], info[1]
-    ids_own, ids_other = own[...], other[0:1]
+    ids_own, ids_other = own[...], other[...]
     first = jnp.where(core == 0, ids_own, ids_other)
     second = jnp.where(core == 0, ids_other, ids_own)
-    before = jnp.where(chip == 0, -1, jnp.where(core == 0, passed[...], other[1:2]))
+    before = jnp.where(chip == 0, -1, jnp.where(core == 0, before_near[...], before_far[...]))
     hots = []
     for ids, low in ((before, TOK - 16), (first, 0), (second, 0)):
         column = jnp.transpose(jnp.broadcast_to(ids, (128, TOK)))[low:]
@@ -232,7 +232,7 @@
     came = lax.ppermute(lax.dynamic_slice_in_dim(out_weight, (1 - core) * cols, cols, axis=1), "seq", swap)
     block = jnp.concatenate([jnp.where(core == 0, mine, came), jnp.where(core == 0, came, mine)], axis=0)
     block, before = tie(block, before)
-    other = lax.ppermute(jnp.concatenate([ids, before], axis=0), "seq", swap)
+    other, passed = lax.ppermute(ids, "seq", swap), lax.ppermute(before, "seq", swap)
     ring = [block, move_z(block, 1), move_z(block, -1)]
 
     ids_block = whole_block((1, TOK))
@@ -241,8 +241,8 @@
     flat = jax.ShapeDtypeStruct((4 * MODES, 128), F32)
     query, base, states, first = call(
         scan_kernel, "scan", info,
-        (ids, other, before, jnp.transpose(table, (1, 0, 2)), short_kernel, poles, residues, skip.reshape(1, -1)),
-        [ids_block, whole_block((2, TOK)), ids_block]
+        (ids, other, before, passed, jnp.transpose(table, (1, 0, 2)), short_kernel, poles, residues, skip.reshape(1, -1)),
+        [ids_block] * 4
         + [core_block((3, vocab, HALF)), core_block((3, 3, HALF)), core_block((MODES, HALF)), core_block((MODES, HALF)), core_block((1, HALF))],
         (jax.ShapeDtypeStruct((2 * TOK, HALF), F32), jax.ShapeDtypeStruct((2 * TOK, HALF), F32), jax.ShapeDtypeStruct((chips, 4 * MODES, 128), BF16), flat),
         (tok_block, tok_block, whole_block((chips, 4 * MODES, 128)), flat_block),
@@ -295,7 +295,7 @@
     partner = lax.ppermute(gated, "seq", swap)
     rows = TOK // n_tp
     tile = part // 2
-    sides = ([], [])
+    sides = []
     for group in weights:
         parts = call(
             functools.partial(project_kernel, ny), "project", info, (gated, partner, *group),
@@ -308,10 +308,10 @@
         total = parts[0].astype(F32)
         for d in range(1, n_tp):
             total = total + lax.ppermute(parts[d], "tp", [(x, (x + d) % n_tp) for x in range(n_tp)]).astype(F32)
-        total = total.astype(BF16)
-        sides[0].append(total[:rows])
-        sides[1].append(lax.ppermute(total[rows:], "seq", swap))
-    return jnp.where(core == 0, jnp.concatenate(sides[0] + sides[1], axis=1), jnp.concatenate(sides[1] + sides[0], axis=1))
+        sides.append(total.astype(BF16))
+    near = jnp.concatenate([total[:rows] for total in sides], axis=1)
+    far = lax.ppermute(jnp.concatenate([total[rows:] for total in sides], axis=1), "seq", swap)
+    return jnp.where(core == 0, jnp.concatenate([near, far], axis=1), jnp.concatenate([far, near], axis=1))
 
 
 def solution(mesh):

time: 107 us -> 107 us (level)
  waiting for transfers between devices: 24.3 us -> 29.1 us
  starting transfers between devices: 61 us -> 56.7 us
    ppermute x3, starting transfers between devices: 13.3 us -> 9.22 us  [the longest x1 6.25 us: body(): lax.ppermute(jnp.concatenate([total[rows:] for total in sides], axis=1),...]
    ppermute x6, waiting for transfers between devices: 0.02 us -> 3.99 us  [body(): lax.ppermute(parts[d], 'tp', [(x, (x + d) % n_tp) for x in range(n_tp)])]
  transfers between devices with their start and end apart: 27 -> 27, of which waited for: 8 -> 11; matrix products, arithmetic and copies ran while one was open for 2% -> 2% of each run, Pallas kernels for 14% -> 14%
where the time goes in v3:
time: 107 us; the launch traced here: 106 us
  starting transfers between devices  56.7 us (53%)
  waiting for transfers between devices  29.1 us (27%)
  Pallas kernels  15.5 us (14%)
  local copies, waits for them, and re-layouts  3.06 us (3%)
  other arithmetic  1.81 us (2%)
    pallas_call x5, Pallas kernels, call(): pl.pallas_call(kernel, grid_spec=pltpu.PrefetchScalarGridSpec(num_scalar_...  15.5 us
    ppermute x6, waiting for transfers between devices, move_y(): lax.ppermute(value, 'seq', [(i, (i + d * 2 * NZ) % n_seq) for i in range(...  14.2 us
    ppermute x8, starting transfers between devices, move_z(): return lax.ppermute(value, 'seq', pairs)  12 us
    ppermute x6, starting transfers between devices, body(): lax.ppermute(parts[d], 'tp', [(x, (x + d) % n_tp) for x in range(n_tp)])  9.78 us
    ppermute x8, waiting for transfers between devices, move_z(): return lax.ppermute(value, 'seq', pairs)  8.11 us
    all_to_all x1, starting transfers between devices, body(): lax.all_to_all(states, 'seq', 0, 0, axis_index_groups=[[2 * p + c for p i...  7.97 us
    ppermute x6, starting transfers between devices, move_y(): lax.ppermute(value, 'seq', [(i, (i + d * 2 * NZ) % n_seq) for i in range(...  6.67 us
    ppermute x1, starting transfers between devices, body(): lax.ppermute(jnp.concatenate([total[rows:] for total in sides], axis=1),...  6.25 us
  transfers between devices with their start and end apart: 27, of which 11 were waited for; matrix products, arithmetic and copies ran while one was open for 2% of the time, Pallas kernels for 14%

profile of v3, /device:TPU:1, one launch (start us, length us, event | category | flops | bytes accessed | tf_op | source)
XLA Modules:
  0.0 106.3 jit_solution(11440016420531924183)
XLA Ops:
  0.0 0.8 constant_dynamic-slice_fusion
  0.8 3.2 %collective-permute-start.1 = (bf16[16,2048]{1,0:T(8,128)(2,1)S(1)}, bf16[16,2048]{1,0:T(8,128)(2,1)S(1)}, u32[]{:S(2)}, u32[]{:S(2)}) collective-permute-start(bf16[16,2048]{1,0:T(8,128)(2,1)S(1)} %constant_dynamic-slice_fusion), channel_id=1, source_target_pairs={{0,4},{4,0},{8,12},{12,8},{16,20},{20,16},{24,28},{28,24},{32,36},... | collective-permute-start | bytes 196616 | tf_op jit(solution)/shard_map/ppermute | solution.py:232
  4.1 1.7 %collective-permute-start.2 = (s32[1,128]{1,0:T(1,128)}, s32[1,128]{1,0:T(1,128)S(1)}, u32[]{:S(2)}, u32[]{:S(2)}) collective-permute-start(s32[1,128]{1,0:T(1,128)} %bitcast.10), channel_id=1, source_target_pairs={{4,8},{12,16},{20,24},{28,32},{36,40},{44,48},{52,56},{60,64},{68,... | collective-permute-start | bytes 1544 | tf_op jit(solution)/shard_map/ppermute | solution.py:229
  5.8 0.0 collective-permute-done.1
  5.8 0.9 broadcast_select_fusion.1
  6.7 0.0 collective-permute-done.2.before_near
  6.7 3.5 %collective-permute-start.5 = (bf16[32,2048]{1,0:T(8,128)(2,1)S(1)}, bf16[32,2048]{1,0:T(8,128)(2,1)S(1)}, u32[]{:S(2)}, u32[]{:S(2)}) collective-permute-start(bf16[32,2048]{1,0:T(8,128)(2,1)S(1)} %pad_maximum_fusion.refs_0_), channel_id=1, source_target_pairs={{0,56},{4,60},{8,0},{12,4},{16,8},{20,12},{24,16},{28,20},{32,24},... | collective-permute-start | bytes 393224 | tf_op jit(solution)/shard_map/ppermute | solution.py:223
  10.2 0.0 collective-permute-start.4
  10.2 3.0 %collective-permute-start = (s32[1,128]{1,0:T(1,128)}, s32[1,128]{1,0:T(1,128)S(1)}, u32[]{:S(2)}, u32[]{:S(2)}) collective-permute-start(s32[1,128]{1,0:T(1,128)} %bitcast.11), channel_id=1, source_target_pairs={{0,4},{4,0},{8,12},{12,8},{16,20},{20,16},{24,28},{28,24},{32,36},... | collective-permute-start | bytes 1544 | tf_op jit(solution)/shard_map/ppermute | solution.py:235
  13.2 0.0 collective-permute-start.3
  13.2 0.7 stack.23.info
  13.9 0.3 collective-permute-done.other
  14.2 0.2 collective-permute-done.3.before_far
  14.3 0.3 copy-done.4
  14.7 0.2 copy-done.5
  14.9 6.0 %scan.1 = (f32[256,512]{1,0:T(8,128)}, f32[256,512]{1,0:T(8,128)}, bf16[32,64,128]{2,1,0:T(8,128)(2,1)}, f32[64,128]{1,0:T(8,128)}) custom-call(s32[5]{0:T(128)} %stack.23.info, s32[1,128]{1,0:T(1,128)} %bitcast.12, s32[1,128]{1,0:T(1,128)} %copy-done.4, s32[1,128]{1,0:T(1,128)} %copy-done.3, s32[1,128]{1,0:T(1,128)} %copy-done.5, ...), custom_call_target="tpu_custom_call" | custom-call | flops 600000000 | bytes 8000000 | tf_op jit(solution)/shard_map/scan/pallas_call | solution.py:192
  20.9 0.0 collective-permute-done.5.refs_2_
  20.9 0.0 collective-permute-done.4.refs_1_
  20.9 0.1 collective-permute-start.6
  21.0 3.0 %collective-permute-start.7 = (bf16[32,2048]{1,0:T(8,128)(2,1)S(1)}, bf16[32,2048]{1,0:T(8,128)(2,1)S(1)}, u32[]{:S(2)}, u32[]{:S(2)}) collective-permute-start(bf16[32,2048]{1,0:T(8,128)(2,1)S(1)} %collective-permute-done.5.refs_2_), channel_id=1, source_target_pairs={{0,56},{4,60},{8,0},{12,4},{16,8},{20,12},{24,16},{28,20},{32,24},... | collective-permute-start | bytes 393224 | tf_op jit(solution)/shard_map/ppermute | solution.py:223
  24.0 3.7 %collective-permute-done.6.refs_3_ = bf16[32,2048]{1,0:T(8,128)(2,1)S(1)} collective-permute-done((bf16[32,2048]{1,0:T(8,128)(2,1)S(1)}, bf16[32,2048]{1,0:T(8,128)(2,1)S(1)}, u32[]{:S(2)}, u32[]{:S(2)}) %collective-permute-start.6) | collective-permute-done | bytes 131104 | tf_op jit(solution)/shard_map/ppermute | solution.py:223
  27.7 0.0 collective-permute-start.8
  27.7 0.0 collective-permute-done.7.refs_4_
  27.7 2.7 %collective-permute-start.9 = (bf16[32,2048]{1,0:T(8,128)(2,1)S(1)}, bf16[32,2048]{1,0:T(8,128)(2,1)S(1)}, u32[]{:S(2)}, u32[]{:S(2)}) collective-permute-start(bf16[32,2048]{1,0:T(8,128)(2,1)S(1)} %collective-permute-done.7.refs_4_), channel_id=1, source_target_pairs={{0,56},{4,60},{8,0},{12,4},{16,8},{20,12},{24,16},{28,20},{32,24},... | collective-permute-start | bytes 393224 | tf_op jit(solution)/shard_map/ppermute | solution.py:223
  30.3 2.9 %collective-permute-done.8.refs_5_ = bf16[32,2048]{1,0:T(8,128)(2,1)S(1)} collective-permute-done((bf16[32,2048]{1,0:T(8,128)(2,1)S(1)}, bf16[32,2048]{1,0:T(8,128)(2,1)S(1)}, u32[]{:S(2)}, u32[]{:S(2)}) %collective-permute-start.8) | collective-permute-done | bytes 131104 | tf_op jit(solution)/shard_map/ppermute | solution.py:223
  33.2 0.0 collective-permute-start.10
  33.2 0.0 collective-permute-done.9.refs_6_
  33.2 2.7 %collective-permute-start.11 = (bf16[32,1024]{1,0:T(8,128)(2,1)S(1)}, bf16[32,1024]{1,0:T(8,128)(2,1)S(1)}, u32[]{:S(2)}, u32[]{:S(2)}) collective-permute-start(bf16[32,1024]{1,0:T(8,128)(2,1)S(1)} %slice.25), channel_id=1, source_target_pairs={{0,56},{4,60},{8,0},{12,4},{16,8},{20,12},{24,16},{28,20},{32,24},... | collective-permute-start | bytes 196616 | tf_op jit(solution)/shard_map/ppermute | solution.py:223
  36.0 1.6 %collective-permute-done.10.refs_7_ = bf16[32,1024]{1,0:T(8,128)(2,1)S(1)} collective-permute-done((bf16[32,1024]{1,0:T(8,128)(2,1)S(1)}, bf16[32,1024]{1,0:T(8,128)(2,1)S(1)}, u32[]{:S(2)}, u32[]{:S(2)}) %collective-permute-start.10) | collective-permute-done | bytes 65568 | tf_op jit(solution)/shard_map/ppermute | solution.py:223
  37.5 0.0 collective-permute-done.11.refs_8_
  37.5 0.6 place.1
  38.2 8.0 %all-to-all-start = ((bf16[32,64,128]{2,1,0:T(8,128)(2,1)}), bf16[32,64,128]{2,1,0:T(8,128)(2,1)}, u32[]{:S(2)}, u32[]{:S(2)}) async-start(bf16[32,64,128]{2,1,0:T(8,128)(2,1)} %get-tuple-element.39), calls=%async_computation | async-start | bytes 1048576 | tf_op jit(solution)/shard_map/all_to_all | solution.py:274
  46.2 1.2 %collective-permute-start.13 = (bf16[256,1024]{1,0:T(8,128)(2,1)S(1)}, bf16[256,1024]{1,0:T(8,128)(2,1)}, u32[]{:S(2)}, u32[]{:S(2)}) collective-permute-start(bf16[256,1024]{1,0:T(8,128)(2,1)S(1)} %get-tuple-element.43.refs_0_), channel_id=1, source_target_pairs={{0,64},{4,68},{8,72},{12,76},{16,80},{20,84},{24,88},{28,92},{32,9... | collective-permute-start | bytes 1572872 | tf_op jit(solution)/shard_map/ppermute | solution.py:219
  47.4 1.5 %collective-permute-start.20 = (bf16[256,1024]{1,0:T(8,128)(2,1)S(1)}, bf16[256,1024]{1,0:T(8,128)(2,1)S(1)}, u32[]{:S(2)}, u32[]{:S(2)}) collective-permute-start(bf16[256,1024]{1,0:T(8,128)(2,1)S(1)} %get-tuple-element.50.refs_0_), channel_id=1, source_target_pairs={{0,192},{4,196},{8,200},{12,204},{16,208},{20,212},{24,216},{28,22... | collective-permute-start | bytes 1572872 | tf_op jit(solution)/shard_map/ppermute | solution.py:219
  48.9 1.2 %collective-permute-start.14 = (bf16[256,1024]{1,0:T(8,128)(2,1)S(1)}, bf16[256,1024]{1,0:T(8,128)(2,1)}, u32[]{:S(2)}, u32[]{:S(2)}) collective-permute-start(bf16[256,1024]{1,0:T(8,128)(2,1)S(1)} %get-tuple-element.43.refs_0_), channel_id=1, source_target_pairs={{0,192},{4,196},{8,200},{12,204},{16,208},{20,212},{24,216},{28,22... | collective-permute-start | bytes 1572872 | tf_op jit(solution)/shard_map/ppermute | solution.py:219
  50.1 13.7 %collective-permute-done.13.refs_1_ = bf16[256,1024]{1,0:T(8,128)(2,1)} collective-permute-done((bf16[256,1024]{1,0:T(8,128)(2,1)S(1)}, bf16[256,1024]{1,0:T(8,128)(2,1)}, u32[]{:S(2)}, u32[]{:S(2)}) %collective-permute-start.13) | collective-permute-done | bytes 524320 | tf_op jit(solution)/shard_map/ppermute | solution.py:219
  63.9 0.0 collective-permute-start.15
  63.9 1.2 %collective-permute-start.19 = (bf16[256,1024]{1,0:T(8,128)(2,1)S(1)}, bf16[256,1024]{1,0:T(8,128)(2,1)}, u32[]{:S(2)}, u32[]{:S(2)}) collective-permute-start(bf16[256,1024]{1,0:T(8,128)(2,1)S(1)} %get-tuple-element.50.refs_0_), channel_id=1, source_target_pairs={{0,64},{4,68},{8,72},{12,76},{16,80},{20,84},{24,88},{28,92},{32,9... | collective-permute-start | bytes 1572872 | tf_op jit(solution)/shard_map/ppermute | solution.py:219
  65.1 0.0 collective-permute-done.20.refs_2_
  65.1 1.5 %collective-permute-start.21 = (bf16[256,1024]{1,0:T(8,128)(2,1)S(1)}, bf16[256,1024]{1,0:T(8,128)(2,1)}, u32[]{:S(2)}, u32[]{:S(2)}) collective-permute-start(bf16[256,1024]{1,0:T(8,128)(2,1)S(1)} %collective-permute-done.20.refs_2_), channel_id=1, source_target_pairs={{0,192},{4,196},{8,200},{12,204},{16,208},{20,212},{24,216},{28,22... | collective-permute-start | bytes 1572872 | tf_op jit(solution)/shard_map/ppermute | solution.py:219
  66.6 3.5 %gate.1.ours = bf16[256,512]{1,0:T(8,128)(2,1)} custom-call(s32[5]{0:T(128)} %stack.23.info, bf16[32,64,128]{2,1,0:T(8,128)(2,1)} %all-to-all-done.states, f32[64,128]{1,0:T(8,128)} %get-tuple-element.40.first, f32[16,1024]{1,0:T(8,128)} %poles.3, f32[16,1024]{1,0:T(8,128)} %residues.3, f32[256,512]{1,0:T(8,128)} %get-tuple-element.41.query, ...), custom_call_target="tpu_custom_call" | custom-call | flops 20000000 | bytes 4000000 | tf_op jit(solution)/shard_map/gate/pallas_call | solution.py:192
  70.1 6.1 %collective-permute-start.12 = (bf16[256,512]{1,0:T(8,128)(2,1)}, bf16[256,512]{1,0:T(8,128)(2,1)S(1)}, u32[]{:S(2)}, u32[]{:S(2)}) collective-permute-start(bf16[256,512]{1,0:T(8,128)(2,1)} %gate.1.ours), channel_id=1, source_target_pairs={{0,4},{4,0},{8,12},{12,8},{16,20},{20,16},{24,28},{28,24},{32,36},... | collective-permute-start | bytes 786440 | tf_op jit(solution)/shard_map/ppermute | solution.py:295
  76.2 0.0 collective-permute-done.14.refs_2_
  76.2 0.0 collective-permute-done.15.refs_3_
  76.2 1.4 %collective-permute-done.12.theirs = bf16[256,512]{1,0:T(8,128)(2,1)S(1)} collective-permute-done((bf16[256,512]{1,0:T(8,128)(2,1)}, bf16[256,512]{1,0:T(8,128)(2,1)S(1)}, u32[]{:S(2)}, u32[]{:S(2)}) %collective-permute-start.12) | collective-permute-done | bytes 262176 | tf_op jit(solution)/shard_map/ppermute | solution.py:295
  77.6 0.9 copy-done
  78.6 2.7 %project.2 = (bf16[64,1024]{1,0:T(8,128)(2,1)S(1)}, bf16[64,1024]{1,0:T(8,128)(2,1)S(1)}, bf16[64,1024]{1,0:T(8,128)(2,1)S(1)}, bf16[64,1024]{1,0:T(8,128)(2,1)S(1)}) custom-call(s32[5]{0:T(128)S(1)} %copy-done.2, bf16[256,512]{1,0:T(8,128)(2,1)S(1)} %copy-done, bf16[256,512]{1,0:T(8,128)(2,1)S(1)} %collective-permute-done.12.theirs, ...), custom_call_target="tpu_custom_call" | custom-call | flops 536870912 | bytes 2097152 | tf_op jit(solution)/shard_map/project/pallas_call | solution.py:192
  81.3 1.3 %collective-permute-start.16 = (bf16[64,1024]{1,0:T(8,128)(2,1)S(1)}, bf16[64,1024]{1,0:T(8,128)(2,1)S(1)}, u32[]{:S(2)}, u32[]{:S(2)}) collective-permute-start(bf16[64,1024]{1,0:T(8,128)(2,1)S(1)} %get-tuple-element.47), channel_id=1, source_target_pairs={{0,1},{1,2},{2,3},{3,0},{4,5},{5,6},{6,7},{7,4},{8,9},{9,10},{10,1... | collective-permute-start | bytes 393224 | tf_op jit(solution)/shard_map/ppermute | solution.py:310
  82.6 2.4 %collective-permute-start.17 = (bf16[64,1024]{1,0:T(8,128)(2,1)S(1)}, bf16[64,1024]{1,0:T(8,128)(2,1)S(1)}, u32[]{:S(2)}, u32[]{:S(2)}) collective-permute-start(bf16[64,1024]{1,0:T(8,128)(2,1)S(1)} %get-tuple-element.48), channel_id=1, source_target_pairs={{0,2},{1,3},{2,0},{3,1},{4,6},{5,7},{6,4},{7,5},{8,10},{9,11},{10,... | collective-permute-start | bytes 393224 | tf_op jit(solution)/shard_map/ppermute | solution.py:310
  85.0 1.2 %collective-permute-start.18 = (bf16[64,1024]{1,0:T(8,128)(2,1)S(1)}, bf16[64,1024]{1,0:T(8,128)(2,1)S(1)}, u32[]{:S(2)}, u32[]{:S(2)}) collective-permute-start(bf16[64,1024]{1,0:T(8,128)(2,1)S(1)} %get-tuple-element.49), channel_id=1, source_target_pairs={{0,3},{1,0},{2,1},{3,2},{4,7},{5,4},{6,5},{7,6},{8,11},{9,8},{10,9... | collective-permute-start | bytes 393224 | tf_op jit(solution)/shard_map/ppermute | solution.py:310
  86.2 0.4 collective-permute-done.19.refs_1_
  86.6 2.6 %project.3 = (bf16[64,1024]{1,0:T(8,128)(2,1)S(1)}, bf16[64,1024]{1,0:T(8,128)(2,1)S(1)}, bf16[64,1024]{1,0:T(8,128)(2,1)S(1)}, bf16[64,1024]{1,0:T(8,128)(2,1)S(1)}) custom-call(s32[5]{0:T(128)S(1)} %copy-done.2, bf16[256,512]{1,0:T(8,128)(2,1)S(1)} %copy-done, bf16[256,512]{1,0:T(8,128)(2,1)S(1)} %collective-permute-done.12.theirs, ...), custom_call_target="tpu_custom_call" | custom-call | flops 536870912 | bytes 2097152 | tf_op jit(solution)/shard_map/project/pallas_call | solution.py:192
  89.2 1.3 %collective-permute-start.22 = (bf16[64,1024]{1,0:T(8,128)(2,1)S(1)}, bf16[64,1024]{1,0:T(8,128)(2,1)S(1)}, u32[]{:S(2)}, u32[]{:S(2)}) collective-permute-start(bf16[64,1024]{1,0:T(8,128)(2,1)S(1)} %get-tuple-element.52), channel_id=1, source_target_pairs={{0,1},{1,2},{2,3},{3,0},{4,5},{5,6},{6,7},{7,4},{8,9},{9,10},{10,1... | collective-permute-start | bytes 393224 | tf_op jit(solution)/shard_map/ppermute | solution.py:310
  90.5 2.5 %collective-permute-start.23 = (bf16[64,1024]{1,0:T(8,128)(2,1)S(1)}, bf16[64,1024]{1,0:T(8,128)(2,1)S(1)}, u32[]{:S(2)}, u32[]{:S(2)}) collective-permute-start(bf16[64,1024]{1,0:T(8,128)(2,1)S(1)} %get-tuple-element.53), channel_id=1, source_target_pairs={{0,2},{1,3},{2,0},{3,1},{4,6},{5,7},{6,4},{7,5},{8,10},{9,11},{10,... | collective-permute-start | bytes 393224 | tf_op jit(solution)/shard_map/ppermute | solution.py:310
  92.9 0.0 collective-permute-done.16
  92.9 1.2 %collective-permute-start.24 = (bf16[64,1024]{1,0:T(8,128)(2,1)S(1)}, bf16[64,1024]{1,0:T(8,128)(2,1)S(1)}, u32[]{:S(2)}, u32[]{:S(2)}) collective-permute-start(bf16[64,1024]{1,0:T(8,128)(2,1)S(1)} %get-tuple-element.54), channel_id=1, source_target_pairs={{0,3},{1,0},{2,1},{3,2},{4,7},{5,4},{6,5},{7,6},{8,11},{9,8},{10,9... | collective-permute-start | bytes 393224 | tf_op jit(solution)/shard_map/ppermute | solution.py:310
  94.1 0.1 add_convert_fusion.1
  94.2 0.9 collective-permute-done.22
  95.1 3.1 %collective-permute-done.23 = bf16[64,1024]{1,0:T(8,128)(2,1)S(1)} collective-permute-done((bf16[64,1024]{1,0:T(8,128)(2,1)S(1)}, bf16[64,1024]{1,0:T(8,128)(2,1)S(1)}, u32[]{:S(2)}, u32[]{:S(2)}) %collective-permute-start.23) | collective-permute-done | bytes 131104 | tf_op jit(solution)/shard_map/ppermute | solution.py:310
  98.2 0.0 collective-permute-done.24
  98.2 0.1 add_convert_fusion
  98.3 6.2 %collective-permute-start.25 = (bf16[32,2048]{1,0:T(8,128)(2,1)S(1)}, bf16[32,2048]{1,0:T(8,128)(2,1)S(1)}, u32[]{:S(2)}, u32[]{:S(2)}) collective-permute-start(bf16[32,2048]{1,0:T(8,128)(2,1)S(1)} %pad_maximum_fusion.1), channel_id=1, source_target_pairs={{0,4},{4,0},{8,12},{12,8},{16,20},{20,16},{24,28},{28,24},{32,36},... | collective-permute-start | bytes 393224 | tf_op jit(solution)/shard_map/ppermute | solution.py:313
  104.5 1.0 collective-permute-done.25
  105.5 0.8 maximum_select_fusion
  (19 shorter events, 0.1 us)
Async XLA Ops:
  0.8 4.9 %collective-permute-start.1 = (bf16[16,2048]{1,0:T(8,128)(2,1)S(1)}, bf16[16,2048]{1,0:T(8,128)(2,1)S(1)}, u32[]{:S(2)}, u32[]{:S(2)}) collective-permute-start(bf16[16,2048]{1,0:T(8,128)(2,1)S(1)} %constant_dynamic-slice_fusion), channel_id=1, source_target_pairs={{0,4},{4,0},{8,12},{12,8},{16,20},{20,16},{24,28},{28,24},{32,36},... | collective-permute-start | bytes 196616 | tf_op jit(solution)/shard_map/ppermute | solution.py:232
  4.1 2.6 %collective-permute-start.2 = (s32[1,128]{1,0:T(1,128)}, s32[1,128]{1,0:T(1,128)S(1)}, u32[]{:S(2)}, u32[]{:S(2)}) collective-permute-start(s32[1,128]{1,0:T(1,128)} %bitcast.10), channel_id=1, source_target_pairs={{4,8},{12,16},{20,24},{28,32},{36,40},{44,48},{52,56},{60,64},{68,... | collective-permute-start | bytes 1544 | tf_op jit(solution)/shard_map/ppermute | solution.py:229
  6.7 7.6 %copy-start.3 = (s32[1,128]{1,0:T(1,128)}, s32[1,128]{1,0:T(1,128)S(1)}, u32[]{:S(2)}) copy-start(s32[1,128]{1,0:T(1,128)S(1)} %collective-permute-done.2.before_near) | copy-start | bytes 1540
  6.7 14.2 %collective-permute-start.5 = (bf16[32,2048]{1,0:T(8,128)(2,1)S(1)}, bf16[32,2048]{1,0:T(8,128)(2,1)S(1)}, u32[]{:S(2)}, u32[]{:S(2)}) collective-permute-start(bf16[32,2048]{1,0:T(8,128)(2,1)S(1)} %pad_maximum_fusion.refs_0_), channel_id=1, source_target_pairs={{0,56},{4,60},{8,0},{12,4},{16,8},{20,12},{24,16},{28,20},{32,24},... | collective-permute-start | bytes 393224 | tf_op jit(solution)/shard_map/ppermute | solution.py:223
  10.2 10.6 %collective-permute-start.4 = (bf16[32,2048]{1,0:T(8,128)(2,1)S(1)}, bf16[32,2048]{1,0:T(8,128)(2,1)S(1)}, u32[]{:S(2)}, u32[]{:S(2)}) collective-permute-start(bf16[32,2048]{1,0:T(8,128)(2,1)S(1)} %pad_maximum_fusion.refs_0_), channel_id=1, source_target_pairs={{0,8},{4,12},{8,16},{12,20},{16,24},{20,28},{24,32},{28,36},{32,40... | collective-permute-start | bytes 393224 | tf_op jit(solution)/shard_map/ppermute | solution.py:223
  10.2 3.9 %collective-permute-start = (s32[1,128]{1,0:T(1,128)}, s32[1,128]{1,0:T(1,128)S(1)}, u32[]{:S(2)}, u32[]{:S(2)}) collective-permute-start(s32[1,128]{1,0:T(1,128)} %bitcast.11), channel_id=1, source_target_pairs={{0,4},{4,0},{8,12},{12,8},{16,20},{20,16},{24,28},{28,24},{32,36},... | collective-permute-start | bytes 1544 | tf_op jit(solution)/shard_map/ppermute | solution.py:235
  13.2 1.1 %collective-permute-start.3 = (s32[1,128]{1,0:T(1,128)S(1)}, s32[1,128]{1,0:T(1,128)S(1)}, u32[]{:S(2)}, u32[]{:S(2)}) collective-permute-start(s32[1,128]{1,0:T(1,128)S(1)} %collective-permute-done.2.before_near), channel_id=1, source_target_pairs={{0,4},{4,0},{8,12},{12,8},{16,20},{20,16},{24,28},{28,24},{32,36},... | collective-permute-start | bytes 1544 | tf_op jit(solution)/shard_map/ppermute | solution.py:235
  13.9 23.7 %copy-start.1 = (s32[5]{0:T(128)S(1)}, s32[5]{0:T(128)}, u32[]{:S(2)}) copy-start(s32[5]{0:T(128)} %stack.23.info) | copy-start | bytes 64
  14.2 0.5 copy-start.4
  14.3 0.6 copy-start.5
  14.9 62.7 %copy-start.2 = (s32[5]{0:T(128)S(1)}, s32[5]{0:T(128)}, u32[]{:S(2)}) copy-start(s32[5]{0:T(128)} %stack.23.info) | copy-start | bytes 64
  20.9 6.8 %collective-permute-start.6 = (bf16[32,2048]{1,0:T(8,128)(2,1)S(1)}, bf16[32,2048]{1,0:T(8,128)(2,1)S(1)}, u32[]{:S(2)}, u32[]{:S(2)}) collective-permute-start(bf16[32,2048]{1,0:T(8,128)(2,1)S(1)} %collective-permute-done.4.refs_1_), channel_id=1, source_target_pairs={{0,8},{4,12},{8,16},{12,20},{16,24},{20,28},{24,32},{28,36},{32,40... | collective-permute-start | bytes 393224 | tf_op jit(solution)/shard_map/ppermute | solution.py:223
  21.0 6.7 %collective-permute-start.7 = (bf16[32,2048]{1,0:T(8,128)(2,1)S(1)}, bf16[32,2048]{1,0:T(8,128)(2,1)S(1)}, u32[]{:S(2)}, u32[]{:S(2)}) collective-permute-start(bf16[32,2048]{1,0:T(8,128)(2,1)S(1)} %collective-permute-done.5.refs_2_), channel_id=1, source_target_pairs={{0,56},{4,60},{8,0},{12,4},{16,8},{20,12},{24,16},{28,20},{32,24},... | collective-permute-start | bytes 393224 | tf_op jit(solution)/shard_map/ppermute | solution.py:223
  27.7 5.5 %collective-permute-start.8 = (bf16[32,2048]{1,0:T(8,128)(2,1)S(1)}, bf16[32,2048]{1,0:T(8,128)(2,1)S(1)}, u32[]{:S(2)}, u32[]{:S(2)}) collective-permute-start(bf16[32,2048]{1,0:T(8,128)(2,1)S(1)} %collective-permute-done.6.refs_3_), channel_id=1, source_target_pairs={{0,8},{4,12},{8,16},{12,20},{16,24},{20,28},{24,32},{28,36},{32,40... | collective-permute-start | bytes 393224 | tf_op jit(solution)/shard_map/ppermute | solution.py:223
  27.7 5.6 %collective-permute-start.9 = (bf16[32,2048]{1,0:T(8,128)(2,1)S(1)}, bf16[32,2048]{1,0:T(8,128)(2,1)S(1)}, u32[]{:S(2)}, u32[]{:S(2)}) collective-permute-start(bf16[32,2048]{1,0:T(8,128)(2,1)S(1)} %collective-permute-done.7.refs_4_), channel_id=1, source_target_pairs={{0,56},{4,60},{8,0},{12,4},{16,8},{20,12},{24,16},{28,20},{32,24},... | collective-permute-start | bytes 393224 | tf_op jit(solution)/shard_map/ppermute | solution.py:223
  33.2 4.3 %collective-permute-start.10 = (bf16[32,1024]{1,0:T(8,128)(2,1)S(1)}, bf16[32,1024]{1,0:T(8,128)(2,1)S(1)}, u32[]{:S(2)}, u32[]{:S(2)}) collective-permute-start(bf16[32,1024]{1,0:T(8,128)(2,1)S(1)} %slice.24), channel_id=1, source_target_pairs={{0,8},{4,12},{8,16},{12,20},{16,24},{20,28},{24,32},{28,36},{32,40... | collective-permute-start | bytes 196616 | tf_op jit(solution)/shard_map/ppermute | solution.py:223
  33.2 4.3 %collective-permute-start.11 = (bf16[32,1024]{1,0:T(8,128)(2,1)S(1)}, bf16[32,1024]{1,0:T(8,128)(2,1)S(1)}, u32[]{:S(2)}, u32[]{:S(2)}) collective-permute-start(bf16[32,1024]{1,0:T(8,128)(2,1)S(1)} %slice.25), channel_id=1, source_target_pairs={{0,56},{4,60},{8,0},{12,4},{16,8},{20,12},{24,16},{28,20},{32,24},... | collective-permute-start | bytes 196616 | tf_op jit(solution)/shard_map/ppermute | solution.py:223
  38.2 28.4 %all-to-all-start = ((bf16[32,64,128]{2,1,0:T(8,128)(2,1)}), bf16[32,64,128]{2,1,0:T(8,128)(2,1)}, u32[]{:S(2)}, u32[]{:S(2)}) async-start(bf16[32,64,128]{2,1,0:T(8,128)(2,1)} %get-tuple-element.39), calls=%async_computation | async-start | bytes 1048576 | tf_op jit(solution)/shard_map/all_to_all | solution.py:274
  46.2 17.7 %collective-permute-start.13 = (bf16[256,1024]{1,0:T(8,128)(2,1)S(1)}, bf16[256,1024]{1,0:T(8,128)(2,1)}, u32[]{:S(2)}, u32[]{:S(2)}) collective-permute-start(bf16[256,1024]{1,0:T(8,128)(2,1)S(1)} %get-tuple-element.43.refs_0_), channel_id=1, source_target_pairs={{0,64},{4,68},{8,72},{12,76},{16,80},{20,84},{24,88},{28,92},{32,9... | collective-permute-start | bytes 1572872 | tf_op jit(solution)/shard_map/ppermute | solution.py:219
  47.4 17.7 %collective-permute-start.20 = (bf16[256,1024]{1,0:T(8,128)(2,1)S(1)}, bf16[256,1024]{1,0:T(8,128)(2,1)S(1)}, u32[]{:S(2)}, u32[]{:S(2)}) collective-permute-start(bf16[256,1024]{1,0:T(8,128)(2,1)S(1)} %get-tuple-element.50.refs_0_), channel_id=1, source_target_pairs={{0,192},{4,196},{8,200},{12,204},{16,208},{20,212},{24,216},{28,22... | collective-permute-start | bytes 1572872 | tf_op jit(solution)/shard_map/ppermute | solution.py:219
  48.9 27.3 %collective-permute-start.14 = (bf16[256,1024]{1,0:T(8,128)(2,1)S(1)}, bf16[256,1024]{1,0:T(8,128)(2,1)}, u32[]{:S(2)}, u32[]{:S(2)}) collective-permute-start(bf16[256,1024]{1,0:T(8,128)(2,1)S(1)} %get-tuple-element.43.refs_0_), channel_id=1, source_target_pairs={{0,192},{4,196},{8,200},{12,204},{16,208},{20,212},{24,216},{28,22... | collective-permute-start | bytes 1572872 | tf_op jit(solution)/shard_map/ppermute | solution.py:219
  63.9 12.4 %collective-permute-start.15 = (bf16[256,1024]{1,0:T(8,128)(2,1)}, bf16[256,1024]{1,0:T(8,128)(2,1)}, u32[]{:S(2)}, u32[]{:S(2)}) collective-permute-start(bf16[256,1024]{1,0:T(8,128)(2,1)} %collective-permute-done.13.refs_1_), channel_id=1, source_target_pairs={{0,64},{4,68},{8,72},{12,76},{16,80},{20,84},{24,88},{28,92},{32,9... | collective-permute-start | bytes 1572872 | tf_op jit(solution)/shard_map/ppermute | solution.py:219
  63.9 22.7 %collective-permute-start.19 = (bf16[256,1024]{1,0:T(8,128)(2,1)S(1)}, bf16[256,1024]{1,0:T(8,128)(2,1)}, u32[]{:S(2)}, u32[]{:S(2)}) collective-permute-start(bf16[256,1024]{1,0:T(8,128)(2,1)S(1)} %get-tuple-element.50.refs_0_), channel_id=1, source_target_pairs={{0,64},{4,68},{8,72},{12,76},{16,80},{20,84},{24,88},{28,92},{32,9... | collective-permute-start | bytes 1572872 | tf_op jit(solution)/shard_map/ppermute | solution.py:219
  65.1 21.5 %collective-permute-start.21 = (bf16[256,1024]{1,0:T(8,128)(2,1)S(1)}, bf16[256,1024]{1,0:T(8,128)(2,1)}, u32[]{:S(2)}, u32[]{:S(2)}) collective-permute-start(bf16[256,1024]{1,0:T(8,128)(2,1)S(1)} %collective-permute-done.20.refs_2_), channel_id=1, source_target_pairs={{0,192},{4,196},{8,200},{12,204},{16,208},{20,212},{24,216},{28,22... | collective-permute-start | bytes 1572872 | tf_op jit(solution)/shard_map/ppermute | solution.py:219
  70.1 7.5 %collective-permute-start.12 = (bf16[256,512]{1,0:T(8,128)(2,1)}, bf16[256,512]{1,0:T(8,128)(2,1)S(1)}, u32[]{:S(2)}, u32[]{:S(2)}) collective-permute-start(bf16[256,512]{1,0:T(8,128)(2,1)} %gate.1.ours), channel_id=1, source_target_pairs={{0,4},{4,0},{8,12},{12,8},{16,20},{20,16},{24,28},{28,24},{32,36},... | collective-permute-start | bytes 786440 | tf_op jit(solution)/shard_map/ppermute | solution.py:295
  77.6 1.0 copy-start
  81.3 11.7 %collective-permute-start.16 = (bf16[64,1024]{1,0:T(8,128)(2,1)S(1)}, bf16[64,1024]{1,0:T(8,128)(2,1)S(1)}, u32[]{:S(2)}, u32[]{:S(2)}) collective-permute-start(bf16[64,1024]{1,0:T(8,128)(2,1)S(1)} %get-tuple-element.47), channel_id=1, source_target_pairs={{0,1},{1,2},{2,3},{3,0},{4,5},{5,6},{6,7},{7,4},{8,9},{9,10},{10,1... | collective-permute-start | bytes 393224 | tf_op jit(solution)/shard_map/ppermute | solution.py:310
  82.6 11.5 %collective-permute-start.17 = (bf16[64,1024]{1,0:T(8,128)(2,1)S(1)}, bf16[64,1024]{1,0:T(8,128)(2,1)S(1)}, u32[]{:S(2)}, u32[]{:S(2)}) collective-permute-start(bf16[64,1024]{1,0:T(8,128)(2,1)S(1)} %get-tuple-element.48), channel_id=1, source_target_pairs={{0,2},{1,3},{2,0},{3,1},{4,6},{5,7},{6,4},{7,5},{8,10},{9,11},{10,... | collective-permute-start | bytes 393224 | tf_op jit(solution)/shard_map/ppermute | solution.py:310
  85.0 9.1 %collective-permute-start.18 = (bf16[64,1024]{1,0:T(8,128)(2,1)S(1)}, bf16[64,1024]{1,0:T(8,128)(2,1)S(1)}, u32[]{:S(2)}, u32[]{:S(2)}) collective-permute-start(bf16[64,1024]{1,0:T(8,128)(2,1)S(1)} %get-tuple-element.49), channel_id=1, source_target_pairs={{0,3},{1,0},{2,1},{3,2},{4,7},{5,4},{6,5},{7,6},{8,11},{9,8},{10,9... | collective-permute-start | bytes 393224 | tf_op jit(solution)/shard_map/ppermute | solution.py:310
  89.2 5.8 %collective-permute-start.22 = (bf16[64,1024]{1,0:T(8,128)(2,1)S(1)}, bf16[64,1024]{1,0:T(8,128)(2,1)S(1)}, u32[]{:S(2)}, u32[]{:S(2)}) collective-permute-start(bf16[64,1024]{1,0:T(8,128)(2,1)S(1)} %get-tuple-element.52), channel_id=1, source_target_pairs={{0,1},{1,2},{2,3},{3,0},{4,5},{5,6},{6,7},{7,4},{8,9},{9,10},{10,1... | collective-permute-start | bytes 393224 | tf_op jit(solution)/shard_map/ppermute | solution.py:310
  90.5 7.7 %collective-permute-start.23 = (bf16[64,1024]{1,0:T(8,128)(2,1)S(1)}, bf16[64,1024]{1,0:T(8,128)(2,1)S(1)}, u32[]{:S(2)}, u32[]{:S(2)}) collective-permute-start(bf16[64,1024]{1,0:T(8,128)(2,1)S(1)} %get-tuple-element.53), channel_id=1, source_target_pairs={{0,2},{1,3},{2,0},{3,1},{4,6},{5,7},{6,4},{7,5},{8,10},{9,11},{10,... | collective-permute-start | bytes 393224 | tf_op jit(solution)/shard_map/ppermute | solution.py:310
  92.9 5.2 %collective-permute-start.24 = (bf16[64,1024]{1,0:T(8,128)(2,1)S(1)}, bf16[64,1024]{1,0:T(8,128)(2,1)S(1)}, u32[]{:S(2)}, u32[]{:S(2)}) collective-permute-start(bf16[64,1024]{1,0:T(8,128)(2,1)S(1)} %get-tuple-element.54), channel_id=1, source_target_pairs={{0,3},{1,0},{2,1},{3,2},{4,7},{5,4},{6,5},{7,6},{8,11},{9,8},{10,9... | collective-permute-start | bytes 393224 | tf_op jit(solution)/shard_map/ppermute | solution.py:310
  98.3 7.2 %collective-permute-start.25 = (bf16[32,2048]{1,0:T(8,128)(2,1)S(1)}, bf16[32,2048]{1,0:T(8,128)(2,1)S(1)}, u32[]{:S(2)}, u32[]{:S(2)}) collective-permute-start(bf16[32,2048]{1,0:T(8,128)(2,1)S(1)} %pad_maximum_fusion.1), channel_id=1, source_target_pairs={{0,4},{4,0},{8,12},{12,8},{16,20},{20,16},{24,28},{28,24},{32,36},... | collective-permute-start | bytes 393224 | tf_op jit(solution)/shard_map/ppermute | solution.py:313
